TPU v7x, 32 devices: a whole 2x2x4 slice. The times are simulated.
32 devices in a mesh: dom: 8 (over z, y), dir: 4 (over x, core).
Axes of the slice: x: 2, y: 2, z: 4, core: 2. Of those that a mesh axis runs over, the one named last changes fastest.
Arguments:
- action: float32 [64, 32, 4096], P('dir', None, 'dom'), may hold values from -6 to 6
- edge_angle: float32 [6, 4096], P(None, 'dom'), may hold values from -3.140625 to 3.140625
- edge_speed: float32 [6, 4096], P(None, 'dom'), may hold values from 0.3 to 3
- neighbours: int32 [6, 4096], P(None, 'dom'), may hold values from 0 to 575, as said below
- send_rows: int32 [2, 256], P(None, 'dom'), may hold values from 0 to 511, as said below
- refract_rate: float32 [32, 4096], P(None, 'dom'), may hold values from -0.45 to 0.45
- refract_angle: float32 [4096], P('dom'), may hold values from -3.140625 to 3.140625
- shift_rate: float32 [32, 4096], P(None, 'dom'), may hold values from -0.45 to 0.45
Outputs:
- wave_action: float32 [64, 32, 4096], P('dir', None, 'dom')
Inputs may be any that keep to these rules, and one draw needn't show every extreme that they name: `neighbours`: slots below 512 are the partition's own nodes, then 32 slots from the lower and 32 from the upper neighbouring partition. `send_rows`: local node numbers within the sending partition.
All inputs are finite; a program needn't handle non-finite values.
Results may differ from a plain program's by a relative error of at most 0.00002.
Values sent between devices are 32-bit elements; how exact they have to be, the bound alone decides.
A program may use at most 64 MiB of HBM per device.

v0:
```python
import math

import jax
import jax.numpy as jnp
from jax import lax
from jax.sharding import PartitionSpec as P

NDIR = 64
NEIGH = 6
SWEEPS = 3


def passed_along(array, axis, by):
    count = lax.axis_size(axis)
    pairs = [(i, i + by) for i in range(count) if 0 <= i + by < count]
    return lax.ppermute(array, axis, pairs)


def extended_2(array, sides, width):
    for axis, dim in sides:
        count, length = (lax.axis_size(axis), array.shape[dim])
        up = [(i, (i + 1) % count) for i in range(count)]
        down = [(j, i) for i, j in up]
        last = lax.slice_in_dim(array, length - width, length, axis=dim)
        first = lax.slice_in_dim(array, 0, width, axis=dim)
        before = lax.ppermute(last, axis, up)
        after = lax.ppermute(first, axis, down)
        array = jnp.concatenate([before, array, after], axis=dim)
    return array


def upwind_freq(refracted, shift_rate):
    padded = jnp.pad(refracted, ((0, 0), (1, 1), (0, 0)))
    rate = shift_rate[None, :, :]
    return refracted - (
        jax.nn.relu(rate) * (refracted - padded[:, :-2, :])
        + jnp.minimum(rate, 0.0) * (padded[:, 2:, :] - refracted)
    )


def shards(
    action, edge_angle, edge_speed, neighbours, send_rows, refract_rate, refract_angle, shift_rate
):
    sector = action.shape[0]
    freq_count = action.shape[1]
    node_count = action.shape[2]
    columns = sector * freq_count
    first_dir = lax.axis_index("dir") * sector
    angles = (
        2.0 * math.pi * (first_dir + jnp.arange(sector, dtype=jnp.int32)).astype(jnp.float32) / NDIR
    )
    weight_nodes = edge_speed[:, :, None] * jax.nn.relu(
        jnp.cos(angles[None, None, :] - edge_angle[:, :, None])
    )
    denom_nodes = 1.0 + jnp.sum(weight_nodes, axis=0)
    weight_wide = jnp.repeat(weight_nodes, freq_count, axis=2)
    denom_wide = jnp.repeat(denom_nodes, freq_count, axis=1)
    start_rows = action.reshape(columns, node_count).T
    field = start_rows
    for sweep in range(SWEEPS):
        down_part = jnp.take(field, send_rows[0], axis=0)
        up_part = jnp.take(field, send_rows[1], axis=0)
        lower_rows = passed_along(up_part, "dom", 1)
        upper_rows = passed_along(down_part, "dom", -1)
        extended = jnp.concatenate([field, lower_rows, upper_rows], axis=0)
        total = start_rows
        for slot in range(NEIGH):
            total = total + weight_wide[slot] * jnp.take(extended, neighbours[slot], axis=0)
        field = total / denom_wide
    swept = field.T.reshape(sector, freq_count, node_count)
    speed = refract_rate[None, :, :] * jnp.sin(angles[:, None, None] - refract_angle[None, None, :])
    padded = extended_2(swept, (("dir", 0),), 1)
    refracted = swept - (
        jax.nn.relu(speed) * (swept - padded[:-2]) + jnp.minimum(speed, 0.0) * (padded[2:] - swept)
    )
    return upwind_freq(refracted, shift_rate)


def solution(mesh):
    return jax.shard_map(
        shards,
        mesh=mesh,
        in_specs=(
            P("dir", None, "dom"),
            P(None, "dom"),
            P(None, "dom"),
            P(None, "dom"),
            P(None, "dom"),
            P(None, "dom"),
            P("dom"),
            P(None, "dom"),
        ),
        out_specs=P("dir", None, "dom"),
        check_vma=False,
    )
```

profile of v0, /device:TPU:17, one launch (start us, length us, event | category | flops | bytes accessed | tf_op | source)
XLA Modules:
  0.0 118.7 jit_solution(2682307887751923103)
XLA Ops:
  0.0 1.6 %copy.17 = f32[512,512]{0,1:T(8,128)S(1)} copy(f32[512,512]{1,0:T(8,128)} %bitcast.54) | data formatting | bytes 2097152 | tf_op jit(solution)/shard_map/reshape | solution.py:58
  2.4 3.1 %collective-permute-start = (f32[32,512]{1,0:T(8,128)S(1)}, f32[32,512]{1,0:T(8,128)S(1)}, u32[]{:S(2)}, u32[]{:S(2)}) collective-permute-start(f32[32,512]{1,0:T(8,128)S(1)} %broadcast_select_fusion.5), channel_id=1, source_target_pairs={{0,4},{4,8},{8,12},{12,16},{16,20},{20,24},{24,28},{1,5},{5,9},{9,... | collective-permute-start | bytes 196616 | tf_op jit(solution)/shard_map/ppermute | solution.py:16
  6.9 3.0 %collective-permute-start.1 = (f32[32,512]{1,0:T(8,128)}, f32[32,512]{1,0:T(8,128)S(1)}, u32[]{:S(2)}, u32[]{:S(2)}) collective-permute-start(f32[32,512]{1,0:T(8,128)} %broadcast_select_fusion.4), channel_id=1, source_target_pairs={{4,0},{8,4},{12,8},{16,12},{20,16},{24,20},{28,24},{5,1},{9,5},{13... | collective-permute-start | bytes 196616 | tf_op jit(solution)/shard_map/ppermute | solution.py:16
  23.0 2.3 %gather_fusion.2 = f32[512,512]{1,0:T(8,128)} fusion(f32[576,512]{1,0:T(8,128)S(1)} %pad_maximum_fusion, s32[1024]{0:T(1024)S(1)} %pad_clamp_fusion.5), kind=kCustom, calls=%fused_computation.1.clone | custom fusion | bytes 2099200 | tf_op jit(solution)/shard_map/jit(_take)/gather | solution.py:68
  25.3 2.4 %gather_fusion.3 = f32[512,512]{1,0:T(8,128)} fusion(f32[576,512]{1,0:T(8,128)S(1)} %pad_maximum_fusion, s32[1024]{0:T(1024)S(1)} %pad_clamp_fusion.4), kind=kCustom, calls=%fused_computation.7.clone | custom fusion | bytes 2099200 | tf_op jit(solution)/shard_map/jit(_take)/gather | solution.py:68
  27.7 2.3 %gather_fusion.4 = f32[512,512]{1,0:T(8,128)} fusion(f32[576,512]{1,0:T(8,128)S(1)} %pad_maximum_fusion, s32[1024]{0:T(1024)S(1)} %pad_clamp_fusion.3), kind=kCustom, calls=%fused_computation.8.clone | custom fusion | bytes 2099200 | tf_op jit(solution)/shard_map/jit(_take)/gather | solution.py:68
  30.0 2.3 %gather_fusion.5 = f32[512,512]{1,0:T(8,128)} fusion(f32[576,512]{1,0:T(8,128)S(1)} %pad_maximum_fusion, s32[1024]{0:T(1024)S(1)} %pad_clamp_fusion.2), kind=kCustom, calls=%fused_computation.9.clone | custom fusion | bytes 2099200 | tf_op jit(solution)/shard_map/jit(_take)/gather | solution.py:68
  32.3 2.3 %gather_fusion.6 = f32[512,512]{1,0:T(8,128)} fusion(f32[576,512]{1,0:T(8,128)S(1)} %pad_maximum_fusion, s32[1024]{0:T(1024)S(1)} %copy-done.4), kind=kCustom, calls=%fused_computation.10.clone | custom fusion | bytes 2099200 | tf_op jit(solution)/shard_map/jit(_take)/gather | solution.py:68
  34.7 2.3 %gather_fusion.7 = f32[512,512]{1,0:T(8,128)} fusion(f32[576,512]{1,0:T(8,128)S(1)} %pad_maximum_fusion, s32[1024]{0:T(1024)S(1)} %pad_clamp_fusion), kind=kCustom, calls=%fused_computation.11.clone | custom fusion | bytes 2099200 | tf_op jit(solution)/shard_map/jit(_take)/gather | solution.py:68
  37.1 5.2 %fusion.28 = f32[512,512]{1,0:T(8,128)S(1)} fusion(f32[512,512]{1,0:T(8,128)} %copy.24, f32[512,512]{1,0:T(8,128)} %copy.23, f32[512,512]{1,0:T(8,128)} %gather_fusion.7, f32[512,512]{1,0:T(8,128)} %copy.22, f32[512,512]{1,0:T(8,128)} %gather_fusion.6, f32[512,512]{1,0:T(8,128)} %copy.21, f32[512,512]{1,0:T(8,128)} %gather_fusion.5, f32[512,512]{1,0:T(8,128)} %copy.20, ...), kind=kLoop, calls=%fused_computation.74 | loop fusion | flops 4980736 | bytes 15731712 | tf_op jit(solution)/shard_map/div | solution.py:69
  43.9 2.2 %collective-permute-start.2 = (f32[32,512]{1,0:T(8,128)S(1)}, f32[32,512]{1,0:T(8,128)S(1)}, u32[]{:S(2)}, u32[]{:S(2)}) collective-permute-start(f32[32,512]{1,0:T(8,128)S(1)} %broadcast_select_fusion.3), channel_id=1, source_target_pairs={{0,4},{4,8},{8,12},{12,16},{16,20},{20,24},{24,28},{1,5},{5,9},{9,... | collective-permute-start | bytes 196616 | tf_op jit(solution)/shard_map/ppermute | solution.py:16
  46.3 4.1 %collective-permute-start.3 = (f32[32,512]{1,0:T(8,128)S(1)}, f32[32,512]{1,0:T(8,128)S(1)}, u32[]{:S(2)}, u32[]{:S(2)}) collective-permute-start(f32[32,512]{1,0:T(8,128)S(1)} %broadcast_select_fusion.2), channel_id=1, source_target_pairs={{4,0},{8,4},{12,8},{16,12},{20,16},{24,20},{28,24},{5,1},{9,5},{13... | collective-permute-start | bytes 196616 | tf_op jit(solution)/shard_map/ppermute | solution.py:16
  50.4 1.8 %collective-permute-done.3 = f32[32,512]{1,0:T(8,128)S(1)} collective-permute-done((f32[32,512]{1,0:T(8,128)S(1)}, f32[32,512]{1,0:T(8,128)S(1)}, u32[]{:S(2)}, u32[]{:S(2)}) %collective-permute-start.3) | collective-permute-done | bytes 65568 | tf_op jit(solution)/shard_map/ppermute | solution.py:16
  53.5 2.3 %gather_fusion.10 = f32[512,512]{1,0:T(8,128)} fusion(f32[576,512]{1,0:T(8,128)S(1)} %pad_maximum_fusion.1, s32[1024]{0:T(1024)S(1)} %pad_clamp_fusion.5), kind=kCustom, calls=%fused_computation.12.clone | custom fusion | bytes 2099200 | tf_op jit(solution)/shard_map/jit(_take)/gather | solution.py:68
  55.9 2.3 %gather_fusion.11 = f32[512,512]{1,0:T(8,128)} fusion(f32[576,512]{1,0:T(8,128)S(1)} %pad_maximum_fusion.1, s32[1024]{0:T(1024)S(1)} %pad_clamp_fusion.4), kind=kCustom, calls=%fused_computation.13.clone | custom fusion | bytes 2099200 | tf_op jit(solution)/shard_map/jit(_take)/gather | solution.py:68
  58.2 2.3 %gather_fusion.12 = f32[512,512]{1,0:T(8,128)} fusion(f32[576,512]{1,0:T(8,128)S(1)} %pad_maximum_fusion.1, s32[1024]{0:T(1024)S(1)} %pad_clamp_fusion.3), kind=kCustom, calls=%fused_computation.14.clone | custom fusion | bytes 2099200 | tf_op jit(solution)/shard_map/jit(_take)/gather | solution.py:68
  60.5 2.4 %gather_fusion.13 = f32[512,512]{1,0:T(8,128)} fusion(f32[576,512]{1,0:T(8,128)S(1)} %pad_maximum_fusion.1, s32[1024]{0:T(1024)S(1)} %pad_clamp_fusion.2), kind=kCustom, calls=%fused_computation.15.clone | custom fusion | bytes 2099200 | tf_op jit(solution)/shard_map/jit(_take)/gather | solution.py:68
  62.9 2.3 %gather_fusion.14 = f32[512,512]{1,0:T(8,128)} fusion(f32[576,512]{1,0:T(8,128)S(1)} %pad_maximum_fusion.1, s32[1024]{0:T(1024)S(1)} %copy-done.4), kind=kCustom, calls=%fused_computation.16.clone | custom fusion | bytes 2099200 | tf_op jit(solution)/shard_map/jit(_take)/gather | solution.py:68
  65.2 2.3 %gather_fusion.15 = f32[512,512]{1,0:T(8,128)} fusion(f32[576,512]{1,0:T(8,128)S(1)} %pad_maximum_fusion.1, s32[1024]{0:T(1024)S(1)} %pad_clamp_fusion), kind=kCustom, calls=%fused_computation.17.clone | custom fusion | bytes 2099200 | tf_op jit(solution)/shard_map/jit(_take)/gather | solution.py:68
  67.6 5.1 %fusion.21 = f32[512,512]{1,0:T(8,128)S(1)} fusion(f32[512,512]{1,0:T(8,128)} %copy.24, f32[512,512]{1,0:T(8,128)} %copy.23, f32[512,512]{1,0:T(8,128)} %gather_fusion.15, f32[512,512]{1,0:T(8,128)} %copy.22, f32[512,512]{1,0:T(8,128)} %gather_fusion.14, f32[512,512]{1,0:T(8,128)} %copy.21, f32[512,512]{1,0:T(8,128)} %gather_fusion.13, f32[512,512]{1,0:T(8,128)} %copy.20, ...), kind=kLoop, calls=%fused_computation.61 | loop fusion | flops 4980736 | bytes 15731712 | tf_op jit(solution)/shard_map/div | solution.py:69
  74.4 4.0 %collective-permute-start.4 = (f32[32,512]{1,0:T(8,128)S(1)}, f32[32,512]{1,0:T(8,128)S(1)}, u32[]{:S(2)}, u32[]{:S(2)}) collective-permute-start(f32[32,512]{1,0:T(8,128)S(1)} %broadcast_select_fusion.1), channel_id=1, source_target_pairs={{0,4},{4,8},{8,12},{12,16},{16,20},{20,24},{24,28},{1,5},{5,9},{9,... | collective-permute-start | bytes 196616 | tf_op jit(solution)/shard_map/ppermute | solution.py:16
  78.5 2.2 %collective-permute-start.5 = (f32[32,512]{1,0:T(8,128)S(1)}, f32[32,512]{1,0:T(8,128)S(1)}, u32[]{:S(2)}, u32[]{:S(2)}) collective-permute-start(f32[32,512]{1,0:T(8,128)S(1)} %broadcast_select_fusion), channel_id=1, source_target_pairs={{4,0},{8,4},{12,8},{16,12},{20,16},{24,20},{28,24},{5,1},{9,5},{13... | collective-permute-start | bytes 196616 | tf_op jit(solution)/shard_map/ppermute | solution.py:16
  80.7 2.9 %collective-permute-done.5 = f32[32,512]{1,0:T(8,128)S(1)} collective-permute-done((f32[32,512]{1,0:T(8,128)S(1)}, f32[32,512]{1,0:T(8,128)S(1)}, u32[]{:S(2)}, u32[]{:S(2)}) %collective-permute-start.5) | collective-permute-done | bytes 65568 | tf_op jit(solution)/shard_map/ppermute | solution.py:16
  84.9 2.3 %gather_fusion.18 = f32[512,512]{1,0:T(8,128)} fusion(f32[576,512]{1,0:T(8,128)S(1)} %pad_maximum_fusion.2, s32[1024]{0:T(1024)S(1)} %pad_clamp_fusion.5), kind=kCustom, calls=%fused_computation.18.clone | custom fusion | bytes 2099200 | tf_op jit(solution)/shard_map/jit(_take)/gather | solution.py:68
  87.2 2.3 %gather_fusion.19 = f32[512,512]{1,0:T(8,128)} fusion(f32[576,512]{1,0:T(8,128)S(1)} %pad_maximum_fusion.2, s32[1024]{0:T(1024)S(1)} %pad_clamp_fusion.4), kind=kCustom, calls=%fused_computation.19.clone | custom fusion | bytes 2099200 | tf_op jit(solution)/shard_map/jit(_take)/gather | solution.py:68
  89.5 2.4 %gather_fusion.20 = f32[512,512]{1,0:T(8,128)} fusion(f32[576,512]{1,0:T(8,128)S(1)} %pad_maximum_fusion.2, s32[1024]{0:T(1024)S(1)} %pad_clamp_fusion.3), kind=kCustom, calls=%fused_computation.20.clone | custom fusion | bytes 2099200 | tf_op jit(solution)/shard_map/jit(_take)/gather | solution.py:68
  91.9 2.3 %gather_fusion.21 = f32[512,512]{1,0:T(8,128)} fusion(f32[576,512]{1,0:T(8,128)S(1)} %pad_maximum_fusion.2, s32[1024]{0:T(1024)S(1)} %pad_clamp_fusion.2), kind=kCustom, calls=%fused_computation.21.clone | custom fusion | bytes 2099200 | tf_op jit(solution)/shard_map/jit(_take)/gather | solution.py:68
  94.2 2.3 %gather_fusion.22 = f32[512,512]{1,0:T(8,128)} fusion(f32[576,512]{1,0:T(8,128)S(1)} %pad_maximum_fusion.2, s32[1024]{0:T(1024)S(1)} %copy-done.4), kind=kCustom, calls=%fused_computation.22.clone | custom fusion | bytes 2099200 | tf_op jit(solution)/shard_map/jit(_take)/gather | solution.py:68
  96.6 2.3 %gather_fusion.23 = f32[512,512]{1,0:T(8,128)} fusion(f32[576,512]{1,0:T(8,128)S(1)} %pad_maximum_fusion.2, s32[1024]{0:T(1024)S(1)} %copy-done.6), kind=kCustom, calls=%fused_computation.23.clone | custom fusion | bytes 2099200 | tf_op jit(solution)/shard_map/jit(_take)/gather | solution.py:68
  98.9 5.1 %fusion.14 = f32[512,512]{0,1:T(8,128)S(1)} fusion(f32[512,512]{1,0:T(8,128)} %copy.24, f32[512,512]{1,0:T(8,128)} %copy.23, f32[512,512]{1,0:T(8,128)} %gather_fusion.23, f32[512,512]{1,0:T(8,128)} %copy.22, f32[512,512]{1,0:T(8,128)} %gather_fusion.22, f32[512,512]{1,0:T(8,128)} %copy.21, f32[512,512]{1,0:T(8,128)} %gather_fusion.21, f32[512,512]{1,0:T(8,128)} %copy.20, ...), kind=kLoop, calls=%fused_computation.48 | loop fusion | flops 4980736 | bytes 15731712 | tf_op jit(solution)/shard_map/transpose | solution.py:70
  104.9 5.1 %collective-permute-start.6 = (f32[1,32,512]{1,2,0:T(8,128)}, f32[1,32,512]{1,2,0:T(8,128)S(1)}, u32[]{:S(2)}, u32[]{:S(2)}) collective-permute-start(f32[1,32,512]{1,2,0:T(8,128)} %get-tuple-element.11), channel_id=1, source_target_pairs={{0,1},{1,2},{2,3},{3,0},{4,5},{5,6},{6,7},{7,4},{8,9},{9,10},{10,1... | collective-permute-start | bytes 196616 | tf_op jit(solution)/shard_map/ppermute | solution.py:26
  110.5 5.3 %collective-permute-done.6 = f32[1,32,512]{1,2,0:T(8,128)S(1)} collective-permute-done((f32[1,32,512]{1,2,0:T(8,128)}, f32[1,32,512]{1,2,0:T(8,128)S(1)}, u32[]{:S(2)}, u32[]{:S(2)}) %collective-permute-start.6) | collective-permute-done | bytes 65568 | tf_op jit(solution)/shard_map/ppermute | solution.py:26
  (120 shorter events, 25.3 us)
Async XLA Ops:
  0.0 1.6 %copy-start.26 = (s32[2,32]{1,0:T(2,128)S(1)}, s32[2,32]{1,0:T(2,128)}, u32[]{:S(2)}) copy-start(s32[2,32]{1,0:T(2,128)} %param.16) | copy-start | bytes 772
  1.6 8.3 %copy-start.9 = (s32[6,512]{1,0:T(8,128)S(1)}, s32[6,512]{1,0:T(8,128)}, u32[]{:S(2)}) copy-start(s32[6,512]{1,0:T(8,128)} %param.15) | copy-start | bytes 36868
  1.6 11.3 %copy-start.7 = (f32[6,512]{1,0:T(8,128)S(1)}, f32[6,512]{1,0:T(8,128)}, u32[]{:S(2)}) copy-start(f32[6,512]{1,0:T(8,128)} %param.13) | copy-start | bytes 36868
  1.6 11.2 %copy-start.8 = (f32[6,512]{1,0:T(8,128)S(1)}, f32[6,512]{1,0:T(8,128)}, u32[]{:S(2)}) copy-start(f32[6,512]{1,0:T(8,128)} %param.14) | copy-start | bytes 36868
  1.6 4.5 %copy-start.16 = (pred[32]{0:T(512)(128)(4,1)}, pred[32]{0:T(512)(128)(4,1)S(1)}, u32[]{:S(2)}) copy-start(pred[32]{0:T(512)(128)(4,1)S(1)} %get-tuple-element.29) | copy-start | bytes 100
  1.7 4.5 %copy-start.18 = (pred[32]{0:T(512)(128)(4,1)}, pred[32]{0:T(512)(128)(4,1)S(1)}, u32[]{:S(2)}) copy-start(pred[32]{0:T(512)(128)(4,1)S(1)} %get-tuple-element.6) | copy-start | bytes 100
  1.7 9.9 %copy-start.21 = (s32[1024]{0:T(1024)}, s32[1024]{0:T(1024)S(1)}, u32[]{:S(2)}) copy-start(s32[1024]{0:T(1024)S(1)} %pad_clamp_fusion.7) | copy-start | bytes 12292
  2.4 20.5 %collective-permute-start = (f32[32,512]{1,0:T(8,128)S(1)}, f32[32,512]{1,0:T(8,128)S(1)}, u32[]{:S(2)}, u32[]{:S(2)}) collective-permute-start(f32[32,512]{1,0:T(8,128)S(1)} %broadcast_select_fusion.5), channel_id=1, source_target_pairs={{0,4},{4,8},{8,12},{12,16},{16,20},{20,24},{24,28},{1,5},{5,9},{9,... | collective-permute-start | bytes 196616 | tf_op jit(solution)/shard_map/ppermute | solution.py:16
  6.9 16.0 %collective-permute-start.1 = (f32[32,512]{1,0:T(8,128)}, f32[32,512]{1,0:T(8,128)S(1)}, u32[]{:S(2)}, u32[]{:S(2)}) collective-permute-start(f32[32,512]{1,0:T(8,128)} %broadcast_select_fusion.4), channel_id=1, source_target_pairs={{4,0},{8,4},{12,8},{16,12},{20,16},{24,20},{28,24},{5,1},{9,5},{13... | collective-permute-start | bytes 196616 | tf_op jit(solution)/shard_map/ppermute | solution.py:16
  22.8 42.4 %copy-start.5 = (s32[1024]{0:T(1024)}, s32[1024]{0:T(1024)S(1)}, u32[]{:S(2)}) copy-start(s32[1024]{0:T(1024)S(1)} %pad_clamp_fusion) | copy-start | bytes 12292
  30.0 2.4 %copy-start.4 = (s32[1024]{0:T(1024)S(1)}, s32[1024]{0:T(1024)}, u32[]{:S(2)}) copy-start(s32[1024]{0:T(1024)} %pad_clamp_fusion.1) | copy-start | bytes 12292
  34.6 2.4 %copy-start.10 = (pred[512]{0:T(512)(128)(4,1)S(1)}, pred[512]{0:T(512)(128)(4,1)}, u32[]{:S(2)}) copy-start(pred[512]{0:T(512)(128)(4,1)} %get-tuple-element.31) | copy-start | bytes 1540
  34.6 2.4 %copy-start.11 = (pred[512]{0:T(512)(128)(4,1)S(1)}, pred[512]{0:T(512)(128)(4,1)}, u32[]{:S(2)}) copy-start(pred[512]{0:T(512)(128)(4,1)} %get-tuple-element.32) | copy-start | bytes 1540
  34.6 2.4 %copy-start.12 = (pred[512]{0:T(512)(128)(4,1)S(1)}, pred[512]{0:T(512)(128)(4,1)}, u32[]{:S(2)}) copy-start(pred[512]{0:T(512)(128)(4,1)} %get-tuple-element.33) | copy-start | bytes 1540
  34.6 2.4 %copy-start.13 = (pred[512]{0:T(512)(128)(4,1)S(1)}, pred[512]{0:T(512)(128)(4,1)}, u32[]{:S(2)}) copy-start(pred[512]{0:T(512)(128)(4,1)} %get-tuple-element.34) | copy-start | bytes 1540
  34.7 2.4 %copy-start.14 = (pred[512]{0:T(512)(128)(4,1)S(1)}, pred[512]{0:T(512)(128)(4,1)}, u32[]{:S(2)}) copy-start(pred[512]{0:T(512)(128)(4,1)} %get-tuple-element.35) | copy-start | bytes 1540
  34.7 2.4 %copy-start.15 = (pred[512]{0:T(512)(128)(4,1)S(1)}, pred[512]{0:T(512)(128)(4,1)}, u32[]{:S(2)}) copy-start(pred[512]{0:T(512)(128)(4,1)} %get-tuple-element.36) | copy-start | bytes 1540
  42.2 8.2 %copy-start.1 = (f32[512,512]{1,0:T(8,128)}, f32[512,512]{1,0:T(8,128)S(1)}, u32[]{:S(2)}) copy-start(f32[512,512]{1,0:T(8,128)S(1)} %fusion.28) | copy-start | bytes 3145732
  42.2 1.6 %copy-start.19 = (pred[32]{0:T(512)(128)(4,1)S(1)}, pred[32]{0:T(512)(128)(4,1)}, u32[]{:S(2)}) copy-start(pred[32]{0:T(512)(128)(4,1)} %copy-done.18) | copy-start | bytes 100
  42.3 3.9 %copy-start.17 = (pred[32]{0:T(512)(128)(4,1)S(1)}, pred[32]{0:T(512)(128)(4,1)}, u32[]{:S(2)}) copy-start(pred[32]{0:T(512)(128)(4,1)} %copy-done.16) | copy-start | bytes 100
  43.9 6.4 %collective-permute-start.2 = (f32[32,512]{1,0:T(8,128)S(1)}, f32[32,512]{1,0:T(8,128)S(1)}, u32[]{:S(2)}, u32[]{:S(2)}) collective-permute-start(f32[32,512]{1,0:T(8,128)S(1)} %broadcast_select_fusion.3), channel_id=1, source_target_pairs={{0,4},{4,8},{8,12},{12,16},{16,20},{20,24},{24,28},{1,5},{5,9},{9,... | collective-permute-start | bytes 196616 | tf_op jit(solution)/shard_map/ppermute | solution.py:16
  46.3 6.0 %collective-permute-start.3 = (f32[32,512]{1,0:T(8,128)S(1)}, f32[32,512]{1,0:T(8,128)S(1)}, u32[]{:S(2)}, u32[]{:S(2)}) collective-permute-start(f32[32,512]{1,0:T(8,128)S(1)} %broadcast_select_fusion.2), channel_id=1, source_target_pairs={{4,0},{8,4},{12,8},{16,12},{20,16},{24,20},{28,24},{5,1},{9,5},{13... | collective-permute-start | bytes 196616 | tf_op jit(solution)/shard_map/ppermute | solution.py:16
  72.7 8.0 %copy-start = (f32[512,512]{1,0:T(8,128)}, f32[512,512]{1,0:T(8,128)S(1)}, u32[]{:S(2)}) copy-start(f32[512,512]{1,0:T(8,128)S(1)} %fusion.21) | copy-start | bytes 3145732
  72.7 7.9 %copy-start.2 = (f32[32,512]{1,0:T(8,128)S(1)}, f32[32,512]{1,0:T(8,128)}, u32[]{:S(2)}) copy-start(f32[32,512]{1,0:T(8,128)} %param.19) | copy-start | bytes 196612
  74.4 6.3 %collective-permute-start.4 = (f32[32,512]{1,0:T(8,128)S(1)}, f32[32,512]{1,0:T(8,128)S(1)}, u32[]{:S(2)}, u32[]{:S(2)}) collective-permute-start(f32[32,512]{1,0:T(8,128)S(1)} %broadcast_select_fusion.1), channel_id=1, source_target_pairs={{0,4},{4,8},{8,12},{12,16},{16,20},{20,24},{24,28},{1,5},{5,9},{9,... | collective-permute-start | bytes 196616 | tf_op jit(solution)/shard_map/ppermute | solution.py:16
  78.5 5.1 %collective-permute-start.5 = (f32[32,512]{1,0:T(8,128)S(1)}, f32[32,512]{1,0:T(8,128)S(1)}, u32[]{:S(2)}, u32[]{:S(2)}) collective-permute-start(f32[32,512]{1,0:T(8,128)S(1)} %broadcast_select_fusion), channel_id=1, source_target_pairs={{4,0},{8,4},{12,8},{16,12},{20,16},{24,20},{28,24},{5,1},{9,5},{13... | collective-permute-start | bytes 196616 | tf_op jit(solution)/shard_map/ppermute | solution.py:16
  94.2 2.4 %copy-start.6 = (s32[1024]{0:T(1024)S(1)}, s32[1024]{0:T(1024)}, u32[]{:S(2)}) copy-start(s32[1024]{0:T(1024)} %copy-done.5) | copy-start | bytes 12292
  98.9 11.1 %copy-start.24 = (f32[16]{0:T(128)S(1)}, f32[16]{0:T(128)}, u32[]{:S(2)}) copy-start(f32[16]{0:T(128)} %copy-done.23) | copy-start | bytes 196
  98.9 11.1 %copy-start.25 = (f32[512]{0:T(512)S(1)}, f32[512]{0:T(512)}, u32[]{:S(2)}) copy-start(f32[512]{0:T(512)} %param.18) | copy-start | bytes 6148
  104.9 11.0 %collective-permute-start.6 = (f32[1,32,512]{1,2,0:T(8,128)}, f32[1,32,512]{1,2,0:T(8,128)S(1)}, u32[]{:S(2)}, u32[]{:S(2)}) collective-permute-start(f32[1,32,512]{1,2,0:T(8,128)} %get-tuple-element.11), channel_id=1, source_target_pairs={{0,1},{1,2},{2,3},{3,0},{4,5},{5,6},{6,7},{7,4},{8,9},{9,10},{10,1... | collective-permute-start | bytes 196616 | tf_op jit(solution)/shard_map/ppermute | solution.py:26
  110.0 7.0 %collective-permute-start.7 = (f32[1,32,512]{1,2,0:T(8,128)S(1)}, f32[1,32,512]{1,2,0:T(8,128)S(1)}, u32[]{:S(2)}, u32[]{:S(2)}) collective-permute-start(f32[1,32,512]{1,2,0:T(8,128)S(1)} %get-tuple-element.12), channel_id=1, source_target_pairs={{1,0},{2,1},{3,2},{0,3},{5,4},{6,5},{7,6},{4,7},{9,8},{10,9},{11,1... | collective-permute-start | bytes 196616 | tf_op jit(solution)/shard_map/ppermute | solution.py:27
  110.2 6.9 %copy-start.3 = (f32[32,512]{1,0:T(8,128)S(1)}, f32[32,512]{1,0:T(8,128)}, u32[]{:S(2)}) copy-start(f32[32,512]{1,0:T(8,128)} %param.17) | copy-start | bytes 196612
  (3 other events, 2.8 us)
where the time goes:
time: 120 us; the launch traced here: 119 us
  local copies, waits for them, and re-layouts  58.6 us (49%)
  other arithmetic  24.7 us (21%)
  starting transfers between devices  23.7 us (20%)
  waiting for transfers between devices  11.1 us (9%)
    gather x18, local copies, waits for them, and re-layouts, shards(): jnp.take(extended, neighbours[slot], axis=0)  42.1 us
    ppermute x6, starting transfers between devices, passed_along(): return lax.ppermute(array, axis, pairs)  18.7 us
    div x2, other arithmetic, shards(): field = total / denom_wide  10.3 us
    broadcast_in_dim x12, local copies, waits for them, and re-layouts, shards(): weight_wide = jnp.repeat(weight_nodes, freq_count, axis=2)  7.69 us
    ppermute x1, waiting for transfers between devices, extended_2(): before = lax.ppermute(last, axis, up)  5.32 us
    transpose x1, other arithmetic, shards(): swept = field.T.reshape(sector, freq_count, node_count)  5.15 us
    ppermute x1, starting transfers between devices, extended_2(): before = lax.ppermute(last, axis, up)  5.08 us
    ppermute x6, waiting for transfers between devices, passed_along(): return lax.ppermute(array, axis, pairs)  4.71 us
  transfers between devices with their start and end apart: 8, of which 4 were waited for; matrix products, arithmetic and copies ran while one was open for 13% of the time, Pallas kernels for 0%

commit v1 on v0

v1 whole, which is shorter than its diff:
```python
import functools
import math

import jax
import jax.numpy as jnp
from jax import lax
from jax.experimental import pallas as pl
from jax.experimental.pallas import tpu as pltpu
from jax.sharding import PartitionSpec as P

NDIR = 64
NEIGH = 6
SWEEPS = 3
LANES = 128
MESH = pl.DeviceIdType.MESH
UNROLL = 8


def kernel(
    sizes, action, edge_angle, edge_speed, neighbours, send_rows, refract_rate, refract_angle, shift_rate,
    out, f0, f1, f2, f3, scaled, weights, columns, swept, bearing, sends, halo,
    send_sem, recv_sem, dir_send, dir_recv,
):
    sector, freqs, nodes, ghost, groups, n_dom, n_dir = sizes
    fields = (f0, f1, f2, f3)
    dom = lax.axis_index("dom")
    here = lax.axis_index("dir")
    has_lower = dom > 0
    has_upper = dom < n_dom - 1
    next_dir = lax.rem(here + 1, n_dir)
    prev_dir = lax.rem(here + n_dir - 1, n_dir)

    barrier = pltpu.get_barrier_semaphore()
    for other in (next_dir, prev_dir):
        pl.semaphore_signal(barrier, inc=1, device_id=(dom, other), device_id_type=MESH)

    @pl.when(has_lower)
    def _():
        pl.semaphore_signal(barrier, inc=1, device_id=(dom - 1, here), device_id_type=MESH)

    @pl.when(has_upper)
    def _():
        pl.semaphore_signal(barrier, inc=1, device_id=(dom + 1, here), device_id_type=MESH)

    low_at, high_at, width = nodes * groups, (nodes + ghost) * groups, ghost * groups

    @pl.when(dom == 0)
    def _():
        for field in (f0, f1, f2):
            field[pl.ds(low_at, width), :] = jnp.zeros((width, LANES), jnp.float32)

    @pl.when(dom == n_dom - 1)
    def _():
        for field in (f0, f1, f2):
            field[pl.ds(high_at, width), :] = jnp.zeros((width, LANES), jnp.float32)

    def to_lower(sweep):
        return pltpu.make_async_remote_copy(
            src_ref=sends.at[sweep, 0], dst_ref=fields[sweep].at[pl.ds(high_at, width)],
            send_sem=send_sem.at[sweep, 0], recv_sem=recv_sem.at[sweep, 0],
            device_id=(dom - 1, here), device_id_type=MESH)

    def to_upper(sweep):
        return pltpu.make_async_remote_copy(
            src_ref=sends.at[sweep, 1], dst_ref=fields[sweep].at[pl.ds(low_at, width)],
            send_sem=send_sem.at[sweep, 1], recv_sem=recv_sem.at[sweep, 1],
            device_id=(dom + 1, here), device_id_type=MESH)

    def start(sweep):
        @pl.when(has_lower)
        def _():
            to_lower(sweep).start()

        @pl.when(has_upper)
        def _():
            to_upper(sweep).start()

    def arrived(sweep):
        @pl.when(has_lower)
        def _():
            to_upper(sweep).wait_recv()

        @pl.when(has_upper)
        def _():
            to_lower(sweep).wait_recv()

    for tile in range(nodes // LANES):
        for group in range(groups):
            block = action[:, group * 8:(group + 1) * 8, tile * LANES:(tile + 1) * LANES]
            turned = block.reshape(LANES, LANES).T
            f0[pl.ds(tile * LANES * groups + group, LANES, stride=groups), :] = turned
            scaled[pl.ds(tile * LANES * groups + group, LANES, stride=groups), :] = turned

    @pl.loop(0, ghost // UNROLL)
    def _(step):
        for u in range(UNROLL):
            at = step * UNROLL + u
            for side in range(2):
                node = send_rows[side, at]
                sends[0, side, pl.ds(at * groups, groups), :] = scaled[pl.ds(node * groups, groups), :]

    pl.semaphore_wait(barrier, 2 + has_lower.astype(jnp.int32) + has_upper.astype(jnp.int32))
    start(0)

    first_dir = here * sector
    turn = 2.0 * math.pi / NDIR
    lane_dir = first_dir + lax.broadcasted_iota(jnp.int32, (8, LANES), 1) // 8
    lane_angle = lane_dir.astype(jnp.float32) * turn
    lane_cos, lane_sin = jnp.cos(lane_angle)[:1], jnp.sin(lane_angle)[:1]
    row_dir = first_dir + lax.broadcasted_iota(jnp.int32, (sector, nodes), 0)
    turned = jnp.sin(row_dir.astype(jnp.float32) * turn - refract_angle[...])
    for d in range(sector):
        bearing[d] = turned[d:d + 1]
    gap = jnp.zeros((8 - NEIGH, nodes), jnp.float32)
    edge_cos = edge_speed[...] * jnp.cos(edge_angle[...])
    edge_sin = edge_speed[...] * jnp.sin(edge_angle[...])
    parts = jnp.concatenate([edge_cos, gap, edge_sin, gap], axis=0)
    columns[...] = parts.T

    rows = 32

    @pl.loop(0, nodes // rows)
    def _(step):
        at = pl.multiple_of(step * rows, rows)
        block = columns[pl.ds(at, rows), :]
        found = []
        total = jnp.ones((rows, LANES), jnp.float32)
        for slot in range(NEIGH):
            weight = jnp.maximum(block[:, slot:slot + 1] * lane_cos + block[:, 8 + slot:9 + slot] * lane_sin, 0.0)
            found.append(weight)
            total = total + weight
        inverse = 1.0 / total
        for slot in range(NEIGH):
            weights[pl.ds(slot * nodes + at, rows), :] = found[slot] * inverse
        for group in range(groups):
            where = pl.ds(at * groups + group, rows, stride=groups)
            scaled[where, :] = scaled[where, :] * inverse

    def update(field, node):
        total = scaled[pl.ds(node * groups, groups), :]
        for slot in range(NEIGH):
            picked = field[pl.ds(neighbours[slot, node] * groups, groups), :]
            total = total + weights[pl.ds(slot * nodes + node, 1), :] * picked
        return total

    for sweep in range(SWEEPS):
        field, result = fields[sweep], fields[sweep + 1]
        arrived(sweep)
        if sweep < SWEEPS - 1:
            @pl.loop(0, ghost // 4)
            def _(step):
                for u in range(4):
                    at = step * 4 + u
                    for side in range(2):
                        sends[sweep + 1, side, pl.ds(at * groups, groups), :] = update(field, send_rows[side, at])

            start(sweep + 1)

        @pl.loop(0, nodes // UNROLL)
        def _(step):
            for u in range(UNROLL):
                node = step * UNROLL + u
                result[pl.ds(node * groups, groups), :] = update(field, node)

    for tile in range(nodes // LANES):
        for group in range(groups):
            block = f3[pl.ds(tile * LANES * groups + group, LANES, stride=groups), :].T
            swept[:, group * 8:(group + 1) * 8, tile * LANES:(tile + 1) * LANES] = block.reshape(sector, 8, LANES)

    up = pltpu.make_async_remote_copy(
        src_ref=swept.at[sector - 1], dst_ref=halo.at[0], send_sem=dir_send.at[0], recv_sem=dir_recv.at[0],
        device_id=(dom, next_dir), device_id_type=MESH)
    down = pltpu.make_async_remote_copy(
        src_ref=swept.at[0], dst_ref=halo.at[1], send_sem=dir_send.at[1], recv_sem=dir_recv.at[1],
        device_id=(dom, prev_dir), device_id_type=MESH)
    up.start()
    down.start()

    freq = lax.broadcasted_iota(jnp.int32, (freqs, LANES), 0)

    def finish(d, before, after):
        for tile in range(nodes // LANES):
            at = pl.ds(tile * LANES, LANES)
            own = swept[d, :, at]
            speed = refract_rate[:, at] * bearing[d, :, at]
            refracted = own - (jnp.maximum(speed, 0.0) * (own - before(at)) + jnp.minimum(speed, 0.0) * (after(at) - own))
            lower = jnp.where(freq == 0, 0.0, pltpu.roll(refracted, 1, 0))
            upper = jnp.where(freq == freqs - 1, 0.0, pltpu.roll(refracted, freqs - 1, 0))
            rate = shift_rate[:, at]
            out[d, :, at] = refracted - (
                jnp.maximum(rate, 0.0) * (refracted - lower) + jnp.minimum(rate, 0.0) * (upper - refracted))

    @pl.loop(1, sector - 1)
    def _(d):
        finish(d, lambda at: swept[d - 1, :, at], lambda at: swept[d + 1, :, at])

    up.wait()
    finish(0, lambda at: halo[0, :, at], lambda at: swept[1, :, at])
    down.wait()
    finish(sector - 1, lambda at: swept[sector - 2, :, at], lambda at: halo[1, :, at])

    for sweep in range(SWEEPS):
        @pl.when(has_lower)
        def _():
            to_lower(sweep).wait_send()

        @pl.when(has_upper)
        def _():
            to_upper(sweep).wait_send()


def shards(
    action, edge_angle, edge_speed, neighbours, send_rows, refract_rate, refract_angle, shift_rate
):
    sector, freqs, nodes = action.shape
    ghost = send_rows.shape[1]
    groups = freqs // 8
    sizes = (sector, freqs, nodes, ghost, groups, lax.axis_size("dom"), lax.axis_size("dir"))
    vmem = pl.BlockSpec(memory_space=pltpu.VMEM)
    smem = pl.BlockSpec(memory_space=pltpu.SMEM)
    field = pltpu.VMEM(((nodes + 2 * ghost) * groups, LANES), jnp.float32)
    local = pltpu.VMEM((nodes * groups, LANES), jnp.float32)
    return pl.pallas_call(
        functools.partial(kernel, sizes),
        out_shape=jax.ShapeDtypeStruct(action.shape, jnp.float32),
        in_specs=[vmem, vmem, vmem, smem, smem, vmem, vmem, vmem],
        out_specs=vmem,
        scratch_shapes=[
            field, field, field, local, local,
            pltpu.VMEM((NEIGH * nodes, LANES), jnp.float32),
            pltpu.VMEM((nodes, 16), jnp.float32),
            pltpu.VMEM((sector, freqs, nodes), jnp.float32),
            pltpu.VMEM((sector, 1, nodes), jnp.float32),
            pltpu.VMEM((SWEEPS, 2, ghost * groups, LANES), jnp.float32),
            pltpu.VMEM((2, freqs, nodes), jnp.float32),
            pltpu.SemaphoreType.DMA((SWEEPS, 2)),
            pltpu.SemaphoreType.DMA((SWEEPS, 2)),
            pltpu.SemaphoreType.DMA((2,)),
            pltpu.SemaphoreType.DMA((2,)),
        ],
        compiler_params=pltpu.CompilerParams(
            collective_id=0, has_side_effects=True, vmem_limit_bytes=32 * 1024 * 1024),
    )(action, edge_angle, edge_speed, neighbours, send_rows, refract_rate,
      refract_angle.reshape(1, nodes), shift_rate)


def solution(mesh):
    return jax.shard_map(
        shards,
        mesh=mesh,
        in_specs=(
            P("dir", None, "dom"),
            P(None, "dom"),
            P(None, "dom"),
            P(None, "dom"),
            P(None, "dom"),
            P(None, "dom"),
            P("dom"),
            P(None, "dom"),
        ),
        out_specs=P("dir", None, "dom"),
        check_vma=False,
    )
```

time: 120 us -> 35.1 us (0.29)
  local copies, waits for them, and re-layouts: 58.6 us -> 7.38 us
  Pallas kernels: 0 us -> 27.2 us
  other arithmetic: 24.7 us -> 0 us
  starting transfers between devices: 23.7 us -> 0 us
  waiting for transfers between devices: 11.1 us -> 0 us
    gather x24 -> x0, local copies, waits for them, and re-layouts: 46.4 us -> none  [the longest x18 42.1 us: shards(): jnp.take(extended, neighbours[slot], axis=0)]
    pallas_call x0 -> x1, Pallas kernels: none -> 27.2 us  [shards(): pl.pallas_call(functools.partial(kernel, sizes), out_shape=jax.ShapeDtype...]
    ppermute x8 -> x0, starting transfers between devices: 23.7 us -> none  [the longest x6 18.7 us: passed_along(): return lax.ppermute(array, axis, pairs)]
    ppermute x8 -> x0, waiting for transfers between devices: 11.1 us -> none  [the longest x1 5.32 us: extended_2(): before = lax.ppermute(last, axis, up)]
    div x3 -> x0, other arithmetic: 10.3 us -> none  [the longest x2 10.3 us: shards(): field = total / denom_wide]
    broadcast_in_dim x13 -> x0, local copies, waits for them, and re-layouts: 7.81 us -> none  [the longest x12 7.69 us: shards(): weight_wide = jnp.repeat(weight_nodes, freq_count, axis=2)]
    unnamed x54 -> x17, local copies, waits for them, and re-layouts: 0.12 us -> 7.38 us
    transpose x1 -> x0, other arithmetic: 5.15 us -> none  [shards(): swept = field.T.reshape(sector, freq_count, node_count)]
  transfers between devices with their start and end apart: 8 -> 0, of which waited for: 4 -> 0; matrix products, arithmetic and copies ran while one was open for 13% -> 0% of each run, Pallas kernels for 0% -> 0%
where the time goes in v1:
time: 35.1 us; the launch traced here: 34.6 us
  Pallas kernels  27.2 us (77%)
  local copies, waits for them, and re-layouts  7.38 us (21%)
    pallas_call x1, Pallas kernels, shards(): pl.pallas_call(functools.partial(kernel, sizes), out_shape=jax.ShapeDtype...  27.2 us
    unnamed x17, local copies, waits for them, and re-layouts  7.38 us

profile of v1, /device:TPU:17, one launch (start us, length us, event | category | flops | bytes accessed | tf_op | source)
XLA Modules:
  0.0 34.6 jit_solution(3181589883563901304)
XLA Ops:
  0.0 0.0 copy-start.7
  0.0 0.7 %copy-done.7 = s32[2,32]{1,0:T(2,128)S(1)} copy-done((s32[2,32]{1,0:T(2,128)S(1)}, s32[2,32]{1,0:T(2,128)}, u32[]{:S(2)}) %copy-start.7) | copy-done | bytes 280
  0.7 0.0 copy-start
  0.7 1.2 %copy-done = f32[16,32,512]{2,1,0:T(8,128)S(1)} copy-done((f32[16,32,512]{2,1,0:T(8,128)S(1)}, f32[16,32,512]{2,1,0:T(8,128)}, u32[]{:S(2)}) %copy-start) | copy-done | bytes 1048600
  1.9 0.0 copy-start.1
  1.9 0.8 %copy-done.1 = f32[32,512]{1,0:T(8,128)S(1)} copy-done((f32[32,512]{1,0:T(8,128)S(1)}, f32[32,512]{1,0:T(8,128)}, u32[]{:S(2)}) %copy-start.1) | copy-done | bytes 65560
  2.7 0.0 copy-start.2
  2.7 0.8 %copy-done.2 = f32[32,512]{1,0:T(8,128)S(1)} copy-done((f32[32,512]{1,0:T(8,128)S(1)}, f32[32,512]{1,0:T(8,128)}, u32[]{:S(2)}) %copy-start.2) | copy-done | bytes 65560
  3.6 0.0 copy-start.3
  3.6 0.7 %copy-done.3 = f32[6,512]{1,0:T(8,128)S(1)} copy-done((f32[6,512]{1,0:T(8,128)S(1)}, f32[6,512]{1,0:T(8,128)}, u32[]{:S(2)}) %copy-start.3) | copy-done | bytes 12312
  4.3 0.0 copy-start.4
  4.3 0.7 %copy-done.4 = f32[6,512]{1,0:T(8,128)S(1)} copy-done((f32[6,512]{1,0:T(8,128)S(1)}, f32[6,512]{1,0:T(8,128)}, u32[]{:S(2)}) %copy-start.4) | copy-done | bytes 12312
  5.0 0.0 copy-start.5
  5.0 0.7 %copy-done.5 = s32[6,512]{1,0:T(8,128)S(1)} copy-done((s32[6,512]{1,0:T(8,128)S(1)}, s32[6,512]{1,0:T(8,128)}, u32[]{:S(2)}) %copy-start.5) | copy-done | bytes 12312
  5.7 0.0 copy-start.6
  5.7 0.7 %copy-done.6 = f32[512]{0:T(512)S(1)} copy-done((f32[512]{0:T(512)S(1)}, f32[512]{0:T(512)}, u32[]{:S(2)}) %copy-start.6) | copy-done | bytes 2072
  6.4 27.2 %shard_map.82 = f32[16,32,512]{2,1,0:T(8,128)S(1)} custom-call(f32[16,32,512]{2,1,0:T(8,128)S(1)} %copy-done, f32[6,512]{1,0:T(8,128)S(1)} %copy-done.3, f32[6,512]{1,0:T(8,128)S(1)} %copy-done.4, s32[6,512]{1,0:T(8,128)S(1)} %copy-done.5, s32[2,32]{1,0:T(2,128)S(1)} %copy-done.7, f32[32,512]{1,0:T(8,128)S(1)} %copy-done.1, f32[1,512]{1,0:T(1,128)S(1)} %bitcast.1, ...), custom_call_target="tpu_custom_call" | custom-call | tf_op jit(solution)/shard_map/pallas_call | solution.py:223
  33.7 1.0 %copy.10 = f32[16,32,512]{2,1,0:T(8,128)} copy(f32[16,32,512]{2,1,0:T(8,128)S(1)} %shard_map.82) | data formatting | bytes 2097152
Async XLA Ops:
  0.0 0.7 %copy-start.7 = (s32[2,32]{1,0:T(2,128)S(1)}, s32[2,32]{1,0:T(2,128)}, u32[]{:S(2)}) copy-start(s32[2,32]{1,0:T(2,128)} %send_rows.1) | copy-start | bytes 772
  0.7 1.2 %copy-start = (f32[16,32,512]{2,1,0:T(8,128)S(1)}, f32[16,32,512]{2,1,0:T(8,128)}, u32[]{:S(2)}) copy-start(f32[16,32,512]{2,1,0:T(8,128)} %action.1) | copy-start | bytes 3145732
  1.9 0.8 %copy-start.1 = (f32[32,512]{1,0:T(8,128)S(1)}, f32[32,512]{1,0:T(8,128)}, u32[]{:S(2)}) copy-start(f32[32,512]{1,0:T(8,128)} %refract_rate.1) | copy-start | bytes 196612
  2.7 0.8 %copy-start.2 = (f32[32,512]{1,0:T(8,128)S(1)}, f32[32,512]{1,0:T(8,128)}, u32[]{:S(2)}) copy-start(f32[32,512]{1,0:T(8,128)} %shift_rate.1) | copy-start | bytes 196612
  3.6 0.7 %copy-start.3 = (f32[6,512]{1,0:T(8,128)S(1)}, f32[6,512]{1,0:T(8,128)}, u32[]{:S(2)}) copy-start(f32[6,512]{1,0:T(8,128)} %edge_angle.1) | copy-start | bytes 36868
  4.3 0.7 %copy-start.4 = (f32[6,512]{1,0:T(8,128)S(1)}, f32[6,512]{1,0:T(8,128)}, u32[]{:S(2)}) copy-start(f32[6,512]{1,0:T(8,128)} %edge_speed.1) | copy-start | bytes 36868
  5.0 0.7 %copy-start.5 = (s32[6,512]{1,0:T(8,128)S(1)}, s32[6,512]{1,0:T(8,128)}, u32[]{:S(2)}) copy-start(s32[6,512]{1,0:T(8,128)} %neighbours.1) | copy-start | bytes 36868
  5.7 0.7 %copy-start.6 = (f32[512]{0:T(512)S(1)}, f32[512]{0:T(512)}, u32[]{:S(2)}) copy-start(f32[512]{0:T(512)} %param.14) | copy-start | bytes 6148

commit v2 on v1

--- a/solution.py
+++ b/solution.py
@@ -14,11 +14,14 @@
 LANES = 128
 MESH = pl.DeviceIdType.MESH
 UNROLL = 8
+BATCH = 32
 
 
 def kernel(
-    sizes, action, edge_angle, edge_speed, neighbours, send_rows, refract_rate, refract_angle, shift_rate,
-    out, f0, f1, f2, f3, scaled, weights, columns, swept, bearing, sends, halo,
+    sizes, action_hbm, edge_angle_hbm, edge_speed_hbm, neighbours_hbm, send_rows_hbm, refract_rate_hbm,
+    refract_angle_hbm, shift_rate_hbm, out_hbm,
+    action, edge_angle, edge_speed, neighbours, send_rows, refract_rate, refract_angle, shift_rate,
+    shared, slots, table, in_sem, out, out_sem, f0, f1, f2, f3, scaled, weights, columns, swept, bearing, sends, halo,
     send_sem, recv_sem, dir_send, dir_recv,
 ):
     sector, freqs, nodes, ghost, groups, n_dom, n_dir = sizes
@@ -30,6 +33,18 @@
     next_dir = lax.rem(here + 1, n_dir)
     prev_dir = lax.rem(here + n_dir - 1, n_dir)
 
+    loads = [
+        pltpu.make_async_copy(source, target, in_sem.at[at]) for at, (source, target) in enumerate((
+            (send_rows_hbm, send_rows), (neighbours_hbm, neighbours), (edge_angle_hbm, edge_angle),
+            (edge_speed_hbm, edge_speed), (refract_angle_hbm, refract_angle),
+            (refract_rate_hbm, refract_rate), (shift_rate_hbm, shift_rate), (neighbours_hbm, shared)))]
+    planes = [
+        pltpu.make_async_copy(
+            action_hbm.at[:, pl.ds(group * 8, 8), :], action.at[:, pl.ds(group * 8, 8), :], in_sem.at[9 + group])
+        for group in range(groups)]
+    for load in loads[:2] + planes + loads[2:]:
+        load.start()
+
     barrier = pltpu.get_barrier_semaphore()
     for other in (next_dir, prev_dir):
         pl.semaphore_signal(barrier, inc=1, device_id=(dom, other), device_id_type=MESH)
@@ -84,12 +99,21 @@
         def _():
             to_lower(sweep).wait_recv()
 
+    loads[1].wait()
+    slots[...] = jnp.zeros_like(slots)
     for tile in range(nodes // LANES):
-        for group in range(groups):
+        slots[tile * 8:tile * 8 + NEIGH, :] = neighbours[:, tile * LANES:(tile + 1) * LANES] * groups
+    to_table = pltpu.make_async_copy(slots, table, in_sem.at[8])
+    to_table.start()
+    for group in range(groups):
+        planes[group].wait()
+        for tile in range(nodes // LANES):
             block = action[:, group * 8:(group + 1) * 8, tile * LANES:(tile + 1) * LANES]
             turned = block.reshape(LANES, LANES).T
             f0[pl.ds(tile * LANES * groups + group, LANES, stride=groups), :] = turned
             scaled[pl.ds(tile * LANES * groups + group, LANES, stride=groups), :] = turned
+
+    loads[0].wait()
 
     @pl.loop(0, ghost // UNROLL)
     def _(step):
@@ -102,6 +126,8 @@
     pl.semaphore_wait(barrier, 2 + has_lower.astype(jnp.int32) + has_upper.astype(jnp.int32))
     start(0)
 
+    for load in loads[2:]:
+        load.wait()
     first_dir = here * sector
     turn = 2.0 * math.pi / NDIR
     lane_dir = first_dir + lax.broadcasted_iota(jnp.int32, (8, LANES), 1) // 8
@@ -136,10 +162,12 @@
             where = pl.ds(at * groups + group, rows, stride=groups)
             scaled[where, :] = scaled[where, :] * inverse
 
-    def update(field, node):
+    to_table.wait()
+
+    def update(field, node, row_of):
         total = scaled[pl.ds(node * groups, groups), :]
         for slot in range(NEIGH):
-            picked = field[pl.ds(neighbours[slot, node] * groups, groups), :]
+            picked = field[pl.ds(row_of(slot), groups), :]
             total = total + weights[pl.ds(slot * nodes + node, 1), :] * picked
         return total
 
@@ -152,15 +180,21 @@
                 for u in range(4):
                     at = step * 4 + u
                     for side in range(2):
-                        sends[sweep + 1, side, pl.ds(at * groups, groups), :] = update(field, send_rows[side, at])
+                        node = send_rows[side, at]
+                        sends[sweep + 1, side, pl.ds(at * groups, groups), :] = update(
+                            field, node, lambda slot: shared[slot, node] * groups)
 
             start(sweep + 1)
 
-        @pl.loop(0, nodes // UNROLL)
-        def _(step):
-            for u in range(UNROLL):
-                node = step * UNROLL + u
-                result[pl.ds(node * groups, groups), :] = update(field, node)
+        @pl.loop(0, nodes // LANES)
+        def _(tile):
+            @pl.loop(0, LANES // BATCH)
+            def _(step):
+                for u in range(BATCH):
+                    lane = step * BATCH + u
+                    node = tile * LANES + lane
+                    result[pl.ds(node * groups, groups), :] = update(
+                        field, node, lambda slot: table[tile * 8 + slot, lane])
 
     for tile in range(nodes // LANES):
         for group in range(groups):
@@ -177,6 +211,9 @@
     down.start()
 
     freq = lax.broadcasted_iota(jnp.int32, (freqs, LANES), 0)
+
+    def stored(d):
+        return pltpu.make_async_copy(out.at[d], out_hbm.at[d], out_sem.at[d])
 
     def finish(d, before, after):
         for tile in range(nodes // LANES):
@@ -190,6 +227,8 @@
             out[d, :, at] = refracted - (
                 jnp.maximum(rate, 0.0) * (refracted - lower) + jnp.minimum(rate, 0.0) * (upper - refracted))
 
+        stored(d).start()
+
     @pl.loop(1, sector - 1)
     def _(d):
         finish(d, lambda at: swept[d - 1, :, at], lambda at: swept[d + 1, :, at])
@@ -207,6 +246,10 @@
         @pl.when(has_upper)
         def _():
             to_upper(sweep).wait_send()
+
+    @pl.loop(0, sector)
+    def _(d):
+        stored(d).wait()
 
 
 def shards(
@@ -216,16 +259,28 @@
     ghost = send_rows.shape[1]
     groups = freqs // 8
     sizes = (sector, freqs, nodes, ghost, groups, lax.axis_size("dom"), lax.axis_size("dir"))
-    vmem = pl.BlockSpec(memory_space=pltpu.VMEM)
-    smem = pl.BlockSpec(memory_space=pltpu.SMEM)
     field = pltpu.VMEM(((nodes + 2 * ghost) * groups, LANES), jnp.float32)
     local = pltpu.VMEM((nodes * groups, LANES), jnp.float32)
     return pl.pallas_call(
         functools.partial(kernel, sizes),
         out_shape=jax.ShapeDtypeStruct(action.shape, jnp.float32),
-        in_specs=[vmem, vmem, vmem, smem, smem, vmem, vmem, vmem],
-        out_specs=vmem,
+        in_specs=[pl.BlockSpec(memory_space=pltpu.HBM)] * 8,
+        out_specs=pl.BlockSpec(memory_space=pltpu.HBM),
         scratch_shapes=[
+            pltpu.VMEM(action.shape, jnp.float32),
+            pltpu.VMEM(edge_angle.shape, jnp.float32),
+            pltpu.VMEM(edge_speed.shape, jnp.float32),
+            pltpu.VMEM(neighbours.shape, jnp.int32),
+            pltpu.SMEM(send_rows.shape, jnp.int32),
+            pltpu.VMEM(refract_rate.shape, jnp.float32),
+            pltpu.VMEM((1, nodes), jnp.float32),
+            pltpu.VMEM(shift_rate.shape, jnp.float32),
+            pltpu.SMEM(neighbours.shape, jnp.int32),
+            pltpu.VMEM((nodes // LANES * 8, LANES), jnp.int32),
+            pltpu.SMEM((nodes // LANES * 8, LANES), jnp.int32),
+            pltpu.SemaphoreType.DMA((9 + groups,)),
+            pltpu.VMEM(action.shape, jnp.float32),
+            pltpu.SemaphoreType.DMA((sector,)),
             field, field, field, local, local,
             pltpu.VMEM((NEIGH * nodes, LANES), jnp.float32),
             pltpu.VMEM((nodes, 16), jnp.float32),
@@ -239,7 +294,7 @@
             pltpu.SemaphoreType.DMA((2,)),
         ],
         compiler_params=pltpu.CompilerParams(
-            collective_id=0, has_side_effects=True, vmem_limit_bytes=32 * 1024 * 1024),
+            collective_id=0, has_side_effects=True, vmem_limit_bytes=64 * 1024 * 1024),
     )(action, edge_angle, edge_speed, neighbours, send_rows, refract_rate,
       refract_angle.reshape(1, nodes), shift_rate)
 

time: 35.1 us -> 29.4 us (0.84)
  local copies, waits for them, and re-layouts: 7.38 us -> 2.29 us
    unnamed x17 -> x1, local copies, waits for them, and re-layouts: 7.38 us -> 2.29 us
where the time goes in v2:
time: 29.4 us; the launch traced here: 29.2 us
  Pallas kernels  26.9 us (91%)
  local copies, waits for them, and re-layouts  2.29 us (8%)
    pallas_call x1, Pallas kernels, shards(): pl.pallas_call(functools.partial(kernel, sizes), out_shape=jax.ShapeDtype...  26.9 us
    unnamed x1, local copies, waits for them, and re-layouts  2.29 us

profile of v2, /device:TPU:17, one launch (start us, length us, event | category | flops | bytes accessed | tf_op | source)
XLA Modules:
  0.0 29.2 jit_solution(4755862193590893879)
XLA Ops:
  0.0 26.9 %shard_map.82 = f32[16,32,512]{2,1,0:T(8,128)} custom-call(f32[16,32,512]{2,1,0:T(8,128)} %action_hbm.1, f32[6,512]{1,0:T(8,128)} %edge_angle_hbm.1, f32[6,512]{1,0:T(8,128)} %edge_speed_hbm.1, s32[6,512]{1,0:T(8,128)} %neighbours_hbm.1, s32[2,32]{1,0:T(2,128)} %send_rows_hbm.1, f32[32,512]{1,0:T(8,128)} %refract_rate_hbm.1, f32[1,512]{1,0:T(1,128)} %bitcast.1, ...), custom_call_target="tpu_custom_call" | custom-call | tf_op jit(solution)/shard_map/pallas_call | solution.py:264
  27.0 2.3 %copy.10 = f32[16,32,512]{2,1,0:T(8,128)} copy(f32[16,32,512]{2,1,0:T(8,128)} %shard_map.82) | data formatting | bytes 2097152

commit v3 on v2

--- a/solution.py
+++ b/solution.py
@@ -19,9 +19,9 @@
 
 def kernel(
     sizes, action_hbm, edge_angle_hbm, edge_speed_hbm, neighbours_hbm, send_rows_hbm, refract_rate_hbm,
-    refract_angle_hbm, shift_rate_hbm, out_hbm,
+    refract_angle_hbm, shift_rate_hbm, out,
     action, edge_angle, edge_speed, neighbours, send_rows, refract_rate, refract_angle, shift_rate,
-    shared, slots, table, in_sem, out, out_sem, f0, f1, f2, f3, scaled, weights, columns, swept, bearing, sends, halo,
+    shared, slots, table, in_sem, f0, f1, f2, f3, scaled, weights, columns, swept, bearing, sends, halo,
     send_sem, recv_sem, dir_send, dir_recv,
 ):
     sector, freqs, nodes, ghost, groups, n_dom, n_dir = sizes
@@ -117,11 +117,12 @@
 
     @pl.loop(0, ghost // UNROLL)
     def _(step):
+        picked = [
+            scaled[pl.ds(send_rows[side, step * UNROLL + u] * groups, groups), :]
+            for u in range(UNROLL) for side in range(2)]
         for u in range(UNROLL):
-            at = step * UNROLL + u
             for side in range(2):
-                node = send_rows[side, at]
-                sends[0, side, pl.ds(at * groups, groups), :] = scaled[pl.ds(node * groups, groups), :]
+                sends[0, side, pl.ds((step * UNROLL + u) * groups, groups), :] = picked[2 * u + side]
 
     pl.semaphore_wait(barrier, 2 + has_lower.astype(jnp.int32) + has_upper.astype(jnp.int32))
     start(0)
@@ -149,6 +150,8 @@
     def _(step):
         at = pl.multiple_of(step * rows, rows)
         block = columns[pl.ds(at, rows), :]
+        places = [pl.ds(at * groups + group, rows, stride=groups) for group in range(groups)]
+        base = [scaled[place, :] for place in places]
         found = []
         total = jnp.ones((rows, LANES), jnp.float32)
         for slot in range(NEIGH):
@@ -159,8 +162,7 @@
         for slot in range(NEIGH):
             weights[pl.ds(slot * nodes + at, rows), :] = found[slot] * inverse
         for group in range(groups):
-            where = pl.ds(at * groups + group, rows, stride=groups)
-            scaled[where, :] = scaled[where, :] * inverse
+            scaled[places[group], :] = base[group] * inverse
 
     to_table.wait()
 
@@ -175,14 +177,16 @@
         field, result = fields[sweep], fields[sweep + 1]
         arrived(sweep)
         if sweep < SWEEPS - 1:
-            @pl.loop(0, ghost // 4)
+            @pl.loop(0, ghost // UNROLL)
             def _(step):
-                for u in range(4):
-                    at = step * 4 + u
+                totals = []
+                for u in range(UNROLL):
                     for side in range(2):
-                        node = send_rows[side, at]
-                        sends[sweep + 1, side, pl.ds(at * groups, groups), :] = update(
-                            field, node, lambda slot: shared[slot, node] * groups)
+                        node = send_rows[side, step * UNROLL + u]
+                        totals.append(update(field, node, lambda slot, node=node: shared[slot, node] * groups))
+                for u in range(UNROLL):
+                    for side in range(2):
+                        sends[sweep + 1, side, pl.ds((step * UNROLL + u) * groups, groups), :] = totals[2 * u + side]
 
             start(sweep + 1)
 
@@ -190,11 +194,14 @@
         def _(tile):
             @pl.loop(0, LANES // BATCH)
             def _(step):
+                totals = []
                 for u in range(BATCH):
                     lane = step * BATCH + u
-                    node = tile * LANES + lane
-                    result[pl.ds(node * groups, groups), :] = update(
-                        field, node, lambda slot: table[tile * 8 + slot, lane])
+                    totals.append(update(
+                        field, tile * LANES + lane, lambda slot, lane=lane: table[tile * 8 + slot, lane]))
+                for u in range(BATCH):
+                    node = tile * LANES + step * BATCH + u
+                    result[pl.ds(node * groups, groups), :] = totals[u]
 
     for tile in range(nodes // LANES):
         for group in range(groups):
@@ -212,22 +219,20 @@
 
     freq = lax.broadcasted_iota(jnp.int32, (freqs, LANES), 0)
 
-    def stored(d):
-        return pltpu.make_async_copy(out.at[d], out_hbm.at[d], out_sem.at[d])
-
     def finish(d, before, after):
-        for tile in range(nodes // LANES):
-            at = pl.ds(tile * LANES, LANES)
+        places = [pl.ds(tile * LANES, LANES) for tile in range(nodes // LANES)]
+        found = []
+        for at in places:
             own = swept[d, :, at]
             speed = refract_rate[:, at] * bearing[d, :, at]
             refracted = own - (jnp.maximum(speed, 0.0) * (own - before(at)) + jnp.minimum(speed, 0.0) * (after(at) - own))
             lower = jnp.where(freq == 0, 0.0, pltpu.roll(refracted, 1, 0))
             upper = jnp.where(freq == freqs - 1, 0.0, pltpu.roll(refracted, freqs - 1, 0))
             rate = shift_rate[:, at]
-            out[d, :, at] = refracted - (
-                jnp.maximum(rate, 0.0) * (refracted - lower) + jnp.minimum(rate, 0.0) * (upper - refracted))
-
-        stored(d).start()
+            found.append(refracted - (
+                jnp.maximum(rate, 0.0) * (refracted - lower) + jnp.minimum(rate, 0.0) * (upper - refracted)))
+        for at, value in zip(places, found):
+            out[d, :, at] = value
 
     @pl.loop(1, sector - 1)
     def _(d):
@@ -246,10 +251,6 @@
         @pl.when(has_upper)
         def _():
             to_upper(sweep).wait_send()
-
-    @pl.loop(0, sector)
-    def _(d):
-        stored(d).wait()
 
 
 def shards(
@@ -263,9 +264,9 @@
     local = pltpu.VMEM((nodes * groups, LANES), jnp.float32)
     return pl.pallas_call(
         functools.partial(kernel, sizes),
-        out_shape=jax.ShapeDtypeStruct(action.shape, jnp.float32),
+        out_shape=pltpu.VMEM(action.shape, jnp.float32),
         in_specs=[pl.BlockSpec(memory_space=pltpu.HBM)] * 8,
-        out_specs=pl.BlockSpec(memory_space=pltpu.HBM),
+        out_specs=pl.BlockSpec(memory_space=pltpu.VMEM),
         scratch_shapes=[
             pltpu.VMEM(action.shape, jnp.float32),
             pltpu.VMEM(edge_angle.shape, jnp.float32),
@@ -279,8 +280,6 @@
             pltpu.VMEM((nodes // LANES * 8, LANES), jnp.int32),
             pltpu.SMEM((nodes // LANES * 8, LANES), jnp.int32),
             pltpu.SemaphoreType.DMA((9 + groups,)),
-            pltpu.VMEM(action.shape, jnp.float32),
-            pltpu.SemaphoreType.DMA((sector,)),
             field, field, field, local, local,
             pltpu.VMEM((NEIGH * nodes, LANES), jnp.float32),
             pltpu.VMEM((nodes, 16), jnp.float32),
@@ -294,7 +293,7 @@
             pltpu.SemaphoreType.DMA((2,)),
         ],
         compiler_params=pltpu.CompilerParams(
-            collective_id=0, has_side_effects=True, vmem_limit_bytes=64 * 1024 * 1024),
+            collective_id=0, has_side_effects=True, vmem_limit_bytes=62 * 1024 * 1024),
     )(action, edge_angle, edge_speed, neighbours, send_rows, refract_rate,
       refract_angle.reshape(1, nodes), shift_rate)
 

time: 29.4 us -> 27.3 us (0.929)
  local copies, waits for them, and re-layouts: 2.29 us -> 0.97 us
  Pallas kernels: 26.9 us -> 26.2 us
    unnamed x1, local copies, waits for them, and re-layouts: 2.29 us -> 0.97 us
    pallas_call x1, Pallas kernels: 26.9 us -> 26.2 us  [shards(): pl.pallas_call(functools.partial(kernel, sizes), out_shape=pltpu.VMEM(act...]
where the time goes in v3:
time: 27.3 us; the launch traced here: 27.1 us
  Pallas kernels  26.2 us (96%)
  local copies, waits for them, and re-layouts  0.97 us (4%)
    pallas_call x1, Pallas kernels, shards(): pl.pallas_call(functools.partial(kernel, sizes), out_shape=pltpu.VMEM(act...  26.2 us
    unnamed x1, local copies, waits for them, and re-layouts  0.97 us

profile of v3, /device:TPU:17, one launch (start us, length us, event | category | flops | bytes accessed | tf_op | source)
XLA Modules:
  0.0 27.1 jit_solution(16395869604040139005)
XLA Ops:
  0.0 26.2 %shard_map.82 = f32[16,32,512]{2,1,0:T(8,128)S(1)} custom-call(f32[16,32,512]{2,1,0:T(8,128)} %action_hbm.1, f32[6,512]{1,0:T(8,128)} %edge_angle_hbm.1, f32[6,512]{1,0:T(8,128)} %edge_speed_hbm.1, s32[6,512]{1,0:T(8,128)} %neighbours_hbm.1, s32[2,32]{1,0:T(2,128)} %send_rows_hbm.1, f32[32,512]{1,0:T(8,128)} %refract_rate_hbm.1, f32[1,512]{1,0:T(1,128)} %bitcast.1, ...), custom_call_target="tpu_custom_call" | custom-call | tf_op jit(solution)/shard_map/pallas_call | solution.py:265
  26.2 1.0 %copy.10 = f32[16,32,512]{2,1,0:T(8,128)} copy(f32[16,32,512]{2,1,0:T(8,128)S(1)} %shard_map.82) | data formatting | bytes 2097152

commit v4 on v3

--- a/solution.py
+++ b/solution.py
@@ -101,8 +101,8 @@
 
     loads[1].wait()
     slots[...] = jnp.zeros_like(slots)
-    for tile in range(nodes // LANES):
-        slots[tile * 8:tile * 8 + NEIGH, :] = neighbours[:, tile * LANES:(tile + 1) * LANES] * groups
+    for step in range(nodes // BATCH):
+        slots[step * 8:step * 8 + NEIGH, :BATCH] = neighbours[:, step * BATCH:(step + 1) * BATCH] * groups
     to_table = pltpu.make_async_copy(slots, table, in_sem.at[8])
     to_table.start()
     for group in range(groups):
@@ -166,11 +166,11 @@
 
     to_table.wait()
 
-    def update(field, node, row_of):
-        total = scaled[pl.ds(node * groups, groups), :]
+    def update(field, start_row, weight_row, extra, row_of):
+        total = scaled[pl.ds(start_row, groups), :]
         for slot in range(NEIGH):
             picked = field[pl.ds(row_of(slot), groups), :]
-            total = total + weights[pl.ds(slot * nodes + node, 1), :] * picked
+            total = total + weights[pl.ds(weight_row + (slot * nodes + extra), 1), :] * picked
         return total
 
     for sweep in range(SWEEPS):
@@ -183,25 +183,25 @@
                 for u in range(UNROLL):
                     for side in range(2):
                         node = send_rows[side, step * UNROLL + u]
-                        totals.append(update(field, node, lambda slot, node=node: shared[slot, node] * groups))
+                        totals.append(update(
+                            field, node * groups, node, 0, lambda slot, node=node: shared[slot, node] * groups))
                 for u in range(UNROLL):
                     for side in range(2):
                         sends[sweep + 1, side, pl.ds((step * UNROLL + u) * groups, groups), :] = totals[2 * u + side]
 
             start(sweep + 1)
 
-        @pl.loop(0, nodes // LANES)
-        def _(tile):
-            @pl.loop(0, LANES // BATCH)
-            def _(step):
-                totals = []
-                for u in range(BATCH):
-                    lane = step * BATCH + u
-                    totals.append(update(
-                        field, tile * LANES + lane, lambda slot, lane=lane: table[tile * 8 + slot, lane]))
-                for u in range(BATCH):
-                    node = tile * LANES + step * BATCH + u
-                    result[pl.ds(node * groups, groups), :] = totals[u]
+        @pl.loop(0, nodes // BATCH)
+        def _(step):
+            first = step * BATCH
+            first_row = step * (BATCH * groups)
+            first_slot = step * 8
+            totals = []
+            for u in range(BATCH):
+                totals.append(update(
+                    field, first_row + u * groups, first, u, lambda slot, u=u: table[first_slot + slot, u]))
+            for u in range(BATCH):
+                result[pl.ds(first_row + u * groups, groups), :] = totals[u]
 
     for tile in range(nodes // LANES):
         for group in range(groups):
@@ -277,8 +277,8 @@
             pltpu.VMEM((1, nodes), jnp.float32),
             pltpu.VMEM(shift_rate.shape, jnp.float32),
             pltpu.SMEM(neighbours.shape, jnp.int32),
-            pltpu.VMEM((nodes // LANES * 8, LANES), jnp.int32),
-            pltpu.SMEM((nodes // LANES * 8, LANES), jnp.int32),
+            pltpu.VMEM((nodes // BATCH * 8, LANES), jnp.int32),
+            pltpu.SMEM((nodes // BATCH * 8, LANES), jnp.int32),
             pltpu.SemaphoreType.DMA((9 + groups,)),
             field, field, field, local, local,
             pltpu.VMEM((NEIGH * nodes, LANES), jnp.float32),

time: 27.3 us -> 24.6 us (0.901)
  Pallas kernels: 26.2 us -> 23.4 us
    pallas_call x1, Pallas kernels: 26.2 us -> 23.4 us  [shards(): pl.pallas_call(functools.partial(kernel, sizes), out_shape=pltpu.VMEM(act...]
where the time goes in v4:
time: 24.6 us; the launch traced here: 24.4 us
  Pallas kernels  23.4 us (95%)
  local copies, waits for them, and re-layouts  0.97 us (4%)
    pallas_call x1, Pallas kernels, shards(): pl.pallas_call(functools.partial(kernel, sizes), out_shape=pltpu.VMEM(act...  23.4 us
    unnamed x1, local copies, waits for them, and re-layouts  0.97 us

profile of v4, /device:TPU:17, one launch (start us, length us, event | category | flops | bytes accessed | tf_op | source)
XLA Modules:
  0.0 24.4 jit_solution(13887543757165525061)
XLA Ops:
  0.0 23.4 %shard_map.82 = f32[16,32,512]{2,1,0:T(8,128)S(1)} custom-call(f32[16,32,512]{2,1,0:T(8,128)} %action_hbm.1, f32[6,512]{1,0:T(8,128)} %edge_angle_hbm.1, f32[6,512]{1,0:T(8,128)} %edge_speed_hbm.1, s32[6,512]{1,0:T(8,128)} %neighbours_hbm.1, s32[2,32]{1,0:T(2,128)} %send_rows_hbm.1, f32[32,512]{1,0:T(8,128)} %refract_rate_hbm.1, f32[1,512]{1,0:T(1,128)} %bitcast.1, ...), custom_call_target="tpu_custom_call" | custom-call | tf_op jit(solution)/shard_map/pallas_call | solution.py:265
  23.4 1.0 %copy.10 = f32[16,32,512]{2,1,0:T(8,128)} copy(f32[16,32,512]{2,1,0:T(8,128)S(1)} %shard_map.82) | data formatting | bytes 2097152

commit v5 on v4

--- a/solution.py
+++ b/solution.py
@@ -173,6 +173,20 @@
             total = total + weights[pl.ds(weight_row + (slot * nodes + extra), 1), :] * picked
         return total
 
+    def to_next(tile):
+        at = pl.ds(pl.multiple_of(tile * LANES, LANES), LANES)
+        return pltpu.make_async_remote_copy(
+            src_ref=swept.at[sector - 1, :, at], dst_ref=halo.at[0, :, at],
+            send_sem=dir_send.at[0, tile], recv_sem=dir_recv.at[0, tile],
+            device_id=(dom, next_dir), device_id_type=MESH)
+
+    def to_prev(tile):
+        at = pl.ds(pl.multiple_of(tile * LANES, LANES), LANES)
+        return pltpu.make_async_remote_copy(
+            src_ref=swept.at[0, :, at], dst_ref=halo.at[1, :, at],
+            send_sem=dir_send.at[1, tile], recv_sem=dir_recv.at[1, tile],
+            device_id=(dom, prev_dir), device_id_type=MESH)
+
     for sweep in range(SWEEPS):
         field, result = fields[sweep], fields[sweep + 1]
         arrived(sweep)
@@ -191,8 +205,7 @@
 
             start(sweep + 1)
 
-        @pl.loop(0, nodes // BATCH)
-        def _(step):
+        def batches(step):
             first = step * BATCH
             first_row = step * (BATCH * groups)
             first_slot = step * 8
@@ -203,19 +216,23 @@
             for u in range(BATCH):
                 result[pl.ds(first_row + u * groups, groups), :] = totals[u]
 
-    for tile in range(nodes // LANES):
-        for group in range(groups):
-            block = f3[pl.ds(tile * LANES * groups + group, LANES, stride=groups), :].T
-            swept[:, group * 8:(group + 1) * 8, tile * LANES:(tile + 1) * LANES] = block.reshape(sector, 8, LANES)
-
-    up = pltpu.make_async_remote_copy(
-        src_ref=swept.at[sector - 1], dst_ref=halo.at[0], send_sem=dir_send.at[0], recv_sem=dir_recv.at[0],
-        device_id=(dom, next_dir), device_id_type=MESH)
-    down = pltpu.make_async_remote_copy(
-        src_ref=swept.at[0], dst_ref=halo.at[1], send_sem=dir_send.at[1], recv_sem=dir_recv.at[1],
-        device_id=(dom, prev_dir), device_id_type=MESH)
-    up.start()
-    down.start()
+        if sweep < SWEEPS - 1:
+            pl.loop(0, nodes // BATCH)(batches)
+        else:
+            @pl.loop(0, nodes // LANES)
+            def _(tile):
+                @pl.loop(0, LANES // BATCH)
+                def _(step):
+                    batches(tile * (LANES // BATCH) + step)
+
+                at = pl.ds(pl.multiple_of(tile * LANES, LANES), LANES)
+                blocks = [
+                    result[pl.ds(tile * (LANES * groups) + group, LANES, stride=groups), :].T
+                    for group in range(groups)]
+                for group in range(groups):
+                    swept[:, group * 8:(group + 1) * 8, at] = blocks[group].reshape(sector, 8, LANES)
+                to_next(tile).start()
+                to_prev(tile).start()
 
     freq = lax.broadcasted_iota(jnp.int32, (freqs, LANES), 0)
 
@@ -238,9 +255,11 @@
     def _(d):
         finish(d, lambda at: swept[d - 1, :, at], lambda at: swept[d + 1, :, at])
 
-    up.wait()
+    for tile in range(nodes // LANES):
+        to_next(tile).wait()
     finish(0, lambda at: halo[0, :, at], lambda at: swept[1, :, at])
-    down.wait()
+    for tile in range(nodes // LANES):
+        to_prev(tile).wait()
     finish(sector - 1, lambda at: swept[sector - 2, :, at], lambda at: halo[1, :, at])
 
     for sweep in range(SWEEPS):
@@ -289,8 +308,8 @@
             pltpu.VMEM((2, freqs, nodes), jnp.float32),
             pltpu.SemaphoreType.DMA((SWEEPS, 2)),
             pltpu.SemaphoreType.DMA((SWEEPS, 2)),
-            pltpu.SemaphoreType.DMA((2,)),
-            pltpu.SemaphoreType.DMA((2,)),
+            pltpu.SemaphoreType.DMA((2, nodes // LANES)),
+            pltpu.SemaphoreType.DMA((2, nodes // LANES)),
         ],
         compiler_params=pltpu.CompilerParams(
             collective_id=0, has_side_effects=True, vmem_limit_bytes=62 * 1024 * 1024),

time: 24.6 us -> 24.3 us (0.988)
  no operation moved by 1% of the time
where the time goes in v5:
time: 24.3 us; the launch traced here: 24.2 us
  Pallas kernels  23.2 us (95%)
  local copies, waits for them, and re-layouts  0.97 us (4%)
    pallas_call x1, Pallas kernels, shards(): pl.pallas_call(functools.partial(kernel, sizes), out_shape=pltpu.VMEM(act...  23.2 us
    unnamed x1, local copies, waits for them, and re-layouts  0.97 us

profile of v5, /device:TPU:17, one launch (start us, length us, event | category | flops | bytes accessed | tf_op | source)
XLA Modules:
  0.0 24.2 jit_solution(16334054750600657908)
XLA Ops:
  0.0 23.2 %shard_map.82 = f32[16,32,512]{2,1,0:T(8,128)S(1)} custom-call(f32[16,32,512]{2,1,0:T(8,128)} %action_hbm.1, f32[6,512]{1,0:T(8,128)} %edge_angle_hbm.1, f32[6,512]{1,0:T(8,128)} %edge_speed_hbm.1, s32[6,512]{1,0:T(8,128)} %neighbours_hbm.1, s32[2,32]{1,0:T(2,128)} %send_rows_hbm.1, f32[32,512]{1,0:T(8,128)} %refract_rate_hbm.1, f32[1,512]{1,0:T(1,128)} %bitcast.1, ...), custom_call_target="tpu_custom_call" | custom-call | tf_op jit(solution)/shard_map/pallas_call | solution.py:284
  23.2 1.0 %copy.10 = f32[16,32,512]{2,1,0:T(8,128)} copy(f32[16,32,512]{2,1,0:T(8,128)S(1)} %shard_map.82) | data formatting | bytes 2097152

commit v6 on v5

--- a/solution.py
+++ b/solution.py
@@ -14,7 +14,8 @@
 LANES = 128
 MESH = pl.DeviceIdType.MESH
 UNROLL = 8
-BATCH = 32
+BATCH = 64
+HALF = 32
 
 
 def kernel(
@@ -105,28 +106,6 @@
         slots[step * 8:step * 8 + NEIGH, :BATCH] = neighbours[:, step * BATCH:(step + 1) * BATCH] * groups
     to_table = pltpu.make_async_copy(slots, table, in_sem.at[8])
     to_table.start()
-    for group in range(groups):
-        planes[group].wait()
-        for tile in range(nodes // LANES):
-            block = action[:, group * 8:(group + 1) * 8, tile * LANES:(tile + 1) * LANES]
-            turned = block.reshape(LANES, LANES).T
-            f0[pl.ds(tile * LANES * groups + group, LANES, stride=groups), :] = turned
-            scaled[pl.ds(tile * LANES * groups + group, LANES, stride=groups), :] = turned
-
-    loads[0].wait()
-
-    @pl.loop(0, ghost // UNROLL)
-    def _(step):
-        picked = [
-            scaled[pl.ds(send_rows[side, step * UNROLL + u] * groups, groups), :]
-            for u in range(UNROLL) for side in range(2)]
-        for u in range(UNROLL):
-            for side in range(2):
-                sends[0, side, pl.ds((step * UNROLL + u) * groups, groups), :] = picked[2 * u + side]
-
-    pl.semaphore_wait(barrier, 2 + has_lower.astype(jnp.int32) + has_upper.astype(jnp.int32))
-    start(0)
-
     for load in loads[2:]:
         load.wait()
     first_dir = here * sector
@@ -143,6 +122,28 @@
     edge_sin = edge_speed[...] * jnp.sin(edge_angle[...])
     parts = jnp.concatenate([edge_cos, gap, edge_sin, gap], axis=0)
     columns[...] = parts.T
+
+    for group in range(groups):
+        planes[group].wait()
+        for tile in range(nodes // LANES):
+            block = action[:, group * 8:(group + 1) * 8, tile * LANES:(tile + 1) * LANES]
+            turned = block.reshape(LANES, LANES).T
+            f0[pl.ds(tile * LANES * groups + group, LANES, stride=groups), :] = turned
+            scaled[pl.ds(tile * LANES * groups + group, LANES, stride=groups), :] = turned
+
+    loads[0].wait()
+
+    @pl.loop(0, ghost // UNROLL)
+    def _(step):
+        picked = [
+            scaled[pl.ds(send_rows[side, step * UNROLL + u] * groups, groups), :]
+            for u in range(UNROLL) for side in range(2)]
+        for u in range(UNROLL):
+            for side in range(2):
+                sends[0, side, pl.ds((step * UNROLL + u) * groups, groups), :] = picked[2 * u + side]
+
+    pl.semaphore_wait(barrier, 2 + has_lower.astype(jnp.int32) + has_upper.astype(jnp.int32))
+    start(0)
 
     rows = 32
 
@@ -209,12 +210,13 @@
             first = step * BATCH
             first_row = step * (BATCH * groups)
             first_slot = step * 8
-            totals = []
-            for u in range(BATCH):
-                totals.append(update(
-                    field, first_row + u * groups, first, u, lambda slot, u=u: table[first_slot + slot, u]))
-            for u in range(BATCH):
-                result[pl.ds(first_row + u * groups, groups), :] = totals[u]
+            for half in range(0, BATCH, HALF):
+                totals = []
+                for u in range(half, half + HALF):
+                    totals.append(update(
+                        field, first_row + u * groups, first, u, lambda slot, u=u: table[first_slot + slot, u]))
+                for u in range(half, half + HALF):
+                    result[pl.ds(first_row + u * groups, groups), :] = totals[u - half]
 
         if sweep < SWEEPS - 1:
             pl.loop(0, nodes // BATCH)(batches)

time: 24.3 us -> 24.9 us (1.025)
  Pallas kernels: 23.2 us -> 23.8 us
    pallas_call x1, Pallas kernels: 23.2 us -> 23.8 us  [shards(): pl.pallas_call(functools.partial(kernel, sizes), out_shape=pltpu.VMEM(act...]
where the time goes in v6:
time: 24.9 us; the launch traced here: 24.7 us
  Pallas kernels  23.8 us (96%)
  local copies, waits for them, and re-layouts  0.97 us (4%)
    pallas_call x1, Pallas kernels, shards(): pl.pallas_call(functools.partial(kernel, sizes), out_shape=pltpu.VMEM(act...  23.8 us
    unnamed x1, local copies, waits for them, and re-layouts  0.97 us

profile of v6, /device:TPU:17, one launch (start us, length us, event | category | flops | bytes accessed | tf_op | source)
XLA Modules:
  0.0 24.7 jit_solution(554772615339792653)
XLA Ops:
  0.0 23.8 %shard_map.82 = f32[16,32,512]{2,1,0:T(8,128)S(1)} custom-call(f32[16,32,512]{2,1,0:T(8,128)} %action_hbm.1, f32[6,512]{1,0:T(8,128)} %edge_angle_hbm.1, f32[6,512]{1,0:T(8,128)} %edge_speed_hbm.1, s32[6,512]{1,0:T(8,128)} %neighbours_hbm.1, s32[2,32]{1,0:T(2,128)} %send_rows_hbm.1, f32[32,512]{1,0:T(8,128)} %refract_rate_hbm.1, f32[1,512]{1,0:T(1,128)} %bitcast.1, ...), custom_call_target="tpu_custom_call" | custom-call | tf_op jit(solution)/shard_map/pallas_call | solution.py:286
  23.8 1.0 %copy.10 = f32[16,32,512]{2,1,0:T(8,128)} copy(f32[16,32,512]{2,1,0:T(8,128)S(1)} %shard_map.82) | data formatting | bytes 2097152

commit v7 on v5

--- a/solution.py
+++ b/solution.py
@@ -21,7 +21,7 @@
     sizes, action_hbm, edge_angle_hbm, edge_speed_hbm, neighbours_hbm, send_rows_hbm, refract_rate_hbm,
     refract_angle_hbm, shift_rate_hbm, out,
     action, edge_angle, edge_speed, neighbours, send_rows, refract_rate, refract_angle, shift_rate,
-    shared, slots, table, in_sem, f0, f1, f2, f3, scaled, weights, columns, swept, bearing, sends, halo,
+    shared, slots, table, in_sem, f0, f1, f2, f3, scaled, weights, columns, swept, bearing, sends,
     send_sem, recv_sem, dir_send, dir_recv,
 ):
     sector, freqs, nodes, ghost, groups, n_dom, n_dir = sizes
@@ -107,11 +107,16 @@
     to_table.start()
     for group in range(groups):
         planes[group].wait()
-        for tile in range(nodes // LANES):
-            block = action[:, group * 8:(group + 1) * 8, tile * LANES:(tile + 1) * LANES]
-            turned = block.reshape(LANES, LANES).T
-            f0[pl.ds(tile * LANES * groups + group, LANES, stride=groups), :] = turned
-            scaled[pl.ds(tile * LANES * groups + group, LANES, stride=groups), :] = turned
+
+    @pl.loop(0, nodes // LANES)
+    def _(tile):
+        at = pl.ds(pl.multiple_of(tile * LANES, LANES), LANES)
+        blocks = [
+            action[:, group * 8:(group + 1) * 8, at].reshape(LANES, LANES).T for group in range(groups)]
+        for group in range(groups):
+            where = pl.ds(tile * (LANES * groups) + group, LANES, stride=groups)
+            f0[where, :] = blocks[group]
+            scaled[where, :] = blocks[group]
 
     loads[0].wait()
 
@@ -176,14 +181,14 @@
     def to_next(tile):
         at = pl.ds(pl.multiple_of(tile * LANES, LANES), LANES)
         return pltpu.make_async_remote_copy(
-            src_ref=swept.at[sector - 1, :, at], dst_ref=halo.at[0, :, at],
+            src_ref=swept.at[sector, :, at], dst_ref=swept.at[0, :, at],
             send_sem=dir_send.at[0, tile], recv_sem=dir_recv.at[0, tile],
             device_id=(dom, next_dir), device_id_type=MESH)
 
     def to_prev(tile):
         at = pl.ds(pl.multiple_of(tile * LANES, LANES), LANES)
         return pltpu.make_async_remote_copy(
-            src_ref=swept.at[0, :, at], dst_ref=halo.at[1, :, at],
+            src_ref=swept.at[1, :, at], dst_ref=swept.at[sector + 1, :, at],
             send_sem=dir_send.at[1, tile], recv_sem=dir_recv.at[1, tile],
             device_id=(dom, prev_dir), device_id_type=MESH)
 
@@ -230,19 +235,19 @@
                     result[pl.ds(tile * (LANES * groups) + group, LANES, stride=groups), :].T
                     for group in range(groups)]
                 for group in range(groups):
-                    swept[:, group * 8:(group + 1) * 8, at] = blocks[group].reshape(sector, 8, LANES)
+                    swept[1:sector + 1, group * 8:(group + 1) * 8, at] = blocks[group].reshape(sector, 8, LANES)
                 to_next(tile).start()
                 to_prev(tile).start()
 
     freq = lax.broadcasted_iota(jnp.int32, (freqs, LANES), 0)
 
-    def finish(d, before, after):
+    def finish(d):
         places = [pl.ds(tile * LANES, LANES) for tile in range(nodes // LANES)]
         found = []
         for at in places:
-            own = swept[d, :, at]
+            own = swept[d + 1, :, at]
             speed = refract_rate[:, at] * bearing[d, :, at]
-            refracted = own - (jnp.maximum(speed, 0.0) * (own - before(at)) + jnp.minimum(speed, 0.0) * (after(at) - own))
+            refracted = own - (jnp.maximum(speed, 0.0) * (own - swept[d, :, at]) + jnp.minimum(speed, 0.0) * (swept[d + 2, :, at] - own))
             lower = jnp.where(freq == 0, 0.0, pltpu.roll(refracted, 1, 0))
             upper = jnp.where(freq == freqs - 1, 0.0, pltpu.roll(refracted, freqs - 1, 0))
             rate = shift_rate[:, at]
@@ -251,16 +256,15 @@
         for at, value in zip(places, found):
             out[d, :, at] = value
 
-    @pl.loop(1, sector - 1)
-    def _(d):
-        finish(d, lambda at: swept[d - 1, :, at], lambda at: swept[d + 1, :, at])
-
-    for tile in range(nodes // LANES):
-        to_next(tile).wait()
-    finish(0, lambda at: halo[0, :, at], lambda at: swept[1, :, at])
-    for tile in range(nodes // LANES):
-        to_prev(tile).wait()
-    finish(sector - 1, lambda at: swept[sector - 2, :, at], lambda at: halo[1, :, at])
+    @pl.loop(0, sector)
+    def _(step):
+        @pl.when(step == sector - 2)
+        def _():
+            for tile in range(nodes // LANES):
+                to_next(tile).wait()
+                to_prev(tile).wait()
+
+        finish(lax.rem(step + 1, sector))
 
     for sweep in range(SWEEPS):
         @pl.when(has_lower)
@@ -302,10 +306,9 @@
             field, field, field, local, local,
             pltpu.VMEM((NEIGH * nodes, LANES), jnp.float32),
             pltpu.VMEM((nodes, 16), jnp.float32),
-            pltpu.VMEM((sector, freqs, nodes), jnp.float32),
+            pltpu.VMEM((sector + 2, freqs, nodes), jnp.float32),
             pltpu.VMEM((sector, 1, nodes), jnp.float32),
             pltpu.VMEM((SWEEPS, 2, ghost * groups, LANES), jnp.float32),
-            pltpu.VMEM((2, freqs, nodes), jnp.float32),
             pltpu.SemaphoreType.DMA((SWEEPS, 2)),
             pltpu.SemaphoreType.DMA((SWEEPS, 2)),
             pltpu.SemaphoreType.DMA((2, nodes // LANES)),

time: 24.3 us -> 24.6 us (1.012)
  Pallas kernels: 23.2 us -> 23.5 us
    pallas_call x1, Pallas kernels: 23.2 us -> 23.5 us  [shards(): pl.pallas_call(functools.partial(kernel, sizes), out_shape=pltpu.VMEM(act...]
where the time goes in v7:
time: 24.6 us; the launch traced here: 24.5 us
  Pallas kernels  23.5 us (96%)
  local copies, waits for them, and re-layouts  0.97 us (4%)
    pallas_call x1, Pallas kernels, shards(): pl.pallas_call(functools.partial(kernel, sizes), out_shape=pltpu.VMEM(act...  23.5 us
    unnamed x1, local copies, waits for them, and re-layouts  0.97 us

profile of v7, /device:TPU:17, one launch (start us, length us, event | category | flops | bytes accessed | tf_op | source)
XLA Modules:
  0.0 24.5 jit_solution(4298814271478308126)
XLA Ops:
  0.0 23.5 %shard_map.82 = f32[16,32,512]{2,1,0:T(8,128)S(1)} custom-call(f32[16,32,512]{2,1,0:T(8,128)} %action_hbm.1, f32[6,512]{1,0:T(8,128)} %edge_angle_hbm.1, f32[6,512]{1,0:T(8,128)} %edge_speed_hbm.1, s32[6,512]{1,0:T(8,128)} %neighbours_hbm.1, s32[2,32]{1,0:T(2,128)} %send_rows_hbm.1, f32[32,512]{1,0:T(8,128)} %refract_rate_hbm.1, f32[1,512]{1,0:T(1,128)} %bitcast.1, ...), custom_call_target="tpu_custom_call" | custom-call | tf_op jit(solution)/shard_map/pallas_call | solution.py:288
  23.5 1.0 %copy.10 = f32[16,32,512]{2,1,0:T(8,128)} copy(f32[16,32,512]{2,1,0:T(8,128)S(1)} %shard_map.82) | data formatting | bytes 2097152

commit v8 on v5

--- a/solution.py
+++ b/solution.py
@@ -110,7 +110,6 @@
         for tile in range(nodes // LANES):
             block = action[:, group * 8:(group + 1) * 8, tile * LANES:(tile + 1) * LANES]
             turned = block.reshape(LANES, LANES).T
-            f0[pl.ds(tile * LANES * groups + group, LANES, stride=groups), :] = turned
             scaled[pl.ds(tile * LANES * groups + group, LANES, stride=groups), :] = turned
 
     loads[0].wait()
@@ -162,6 +161,7 @@
         for slot in range(NEIGH):
             weights[pl.ds(slot * nodes + at, rows), :] = found[slot] * inverse
         for group in range(groups):
+            f0[places[group], :] = base[group]
             scaled[places[group], :] = base[group] * inverse
 
     to_table.wait()

time: 24.3 us -> 24.3 us (level)
  no operation moved by 1% of the time
where the time goes in v8:
time: 24.3 us; the launch traced here: 24.2 us
  Pallas kernels  23.2 us (95%)
  local copies, waits for them, and re-layouts  0.97 us (4%)
    pallas_call x1, Pallas kernels, shards(): pl.pallas_call(functools.partial(kernel, sizes), out_shape=pltpu.VMEM(act...  23.2 us
    unnamed x1, local copies, waits for them, and re-layouts  0.97 us

profile of v8, /device:TPU:17, one launch (start us, length us, event | category | flops | bytes accessed | tf_op | source)
XLA Modules:
  0.0 24.2 jit_solution(10470341433814257017)
XLA Ops:
  0.0 23.2 %shard_map.82 = f32[16,32,512]{2,1,0:T(8,128)S(1)} custom-call(f32[16,32,512]{2,1,0:T(8,128)} %action_hbm.1, f32[6,512]{1,0:T(8,128)} %edge_angle_hbm.1, f32[6,512]{1,0:T(8,128)} %edge_speed_hbm.1, s32[6,512]{1,0:T(8,128)} %neighbours_hbm.1, s32[2,32]{1,0:T(2,128)} %send_rows_hbm.1, f32[32,512]{1,0:T(8,128)} %refract_rate_hbm.1, f32[1,512]{1,0:T(1,128)} %bitcast.1, ...), custom_call_target="tpu_custom_call" | custom-call | tf_op jit(solution)/shard_map/pallas_call | solution.py:284
  23.2 1.0 %copy.10 = f32[16,32,512]{2,1,0:T(8,128)} copy(f32[16,32,512]{2,1,0:T(8,128)S(1)} %shard_map.82) | data formatting | bytes 2097152
